TPU v7x, 128 devices: a whole 4x4x4 slice. The times are simulated.
128 devices in a mesh: seq: 8 (over y_lo, x), table: 16 (over z, y_hi, core).
Axes of the slice: x: 4, y: 4 (y_hi: 2, y_lo: 2; y = y_hi * 2 + y_lo), z: 4, core: 2. Of those that a mesh axis runs over, the one named last changes fastest.
Arguments:
- item_table: bfloat16 [262144, 512], P(('seq', 'table')), may hold values from -6 to 6
- owner: int32 [16, 4096, 1], P('table', 'seq'), may hold values from 0 to 127; in each aligned block of 512 rows (0 to 511, 512 to 1023, ..., all dimensions but the last counted through in order) at most 8 rows name the same one
- item_row: int32 [16, 4096], P('table', 'seq'), may hold values from 0 to 2047
- lengths: int32 [16], P('table'), may hold values from 1 to 4096, as said below
- gain_in: float32 [512], replicated, may hold values from 0.5 to 1.5
- gain_out: float32 [512], replicated, may hold values from 0.5 to 1.5
- w_in: bfloat16 [512, 2048], replicated, may hold values from -0.25 to 0.25
- w_out: bfloat16 [512, 512], replicated, may hold values from -0.25 to 0.25
- out_grad: bfloat16 [16, 4096, 512], P('table', 'seq'), may hold values from -6 to 6
Outputs:
- hidden_out: bfloat16 [16, 4096, 512], P('table', 'seq')
- table_grad: float32 [262144, 512], P(('seq', 'table'))
- w_in_grad: float32 [512, 2048], replicated
- w_out_grad: float32 [512, 512], replicated
Inputs may be any that keep to these rules, and one draw needn't show every extreme that they name: Among the 512 events of one device (positions s*512 to (s+1)*512 - 1 of one user), no owner appears more than 8 times, and some device's block reaches 8. `lengths`: at least one history has all 4096 events live.
All inputs are finite; a program needn't handle non-finite values.
Results may differ from a plain program's by a relative error of at most 0.0083.
Values may be sent and summed in bfloat16 or wider, within the bound.
A program may use at most 128 MiB of HBM per device.

v0:
```python
import jax
import jax.numpy as jnp
from jax import lax
from jax.sharding import PartitionSpec as P

HEADS = 4
HEAD = 128


def layer_norm(rows, gain):
    mean = jnp.mean(rows, -1, keepdims=True)
    centred = rows - mean
    variance = jnp.mean(centred * centred, -1, keepdims=True)
    return centred * lax.rsqrt(variance + 1e-05) * gain


def slope(values):
    sigma = jax.nn.sigmoid(values)
    return sigma * (1.0 + values * (1.0 - sigma))


def split_heads(rows):
    return rows.reshape(rows.shape[0], HEADS, HEAD)


def scores_mask(queries, keys, query_pos, key_pos, length):
    scores = jnp.einsum(
        "ihd,jhd->hij", split_heads(queries), split_heads(keys), preferred_element_type=jnp.float32
    ) * HEAD ** (-0.5)
    allowed = (
        (key_pos[None, :] <= query_pos[:, None])
        & (key_pos[None, :] < length)
        & (query_pos[:, None] < length)
    )
    return (scores, allowed.astype(jnp.float32)[None])


def attn_weights(scores, allowed):
    return (jax.nn.silu(scores) * allowed).astype(jnp.bfloat16)


def attend(queries, keys, values, query_pos, key_pos, length):
    scores, allowed = scores_mask(queries, keys, query_pos, key_pos, length)
    weights = attn_weights(scores, allowed)
    mixed = jnp.einsum(
        "hij,jhd->ihd", weights, split_heads(values), preferred_element_type=jnp.float32
    )
    return mixed.reshape(queries.shape[0], -1)


def query_grad(queries, keys, values, out_back, query_pos, key_pos, length):
    scores, allowed = scores_mask(queries, keys, query_pos, key_pos, length)
    pulled = jnp.einsum(
        "ihd,jhd->hij",
        split_heads(out_back),
        split_heads(values),
        preferred_element_type=jnp.float32,
    )
    score_back = (pulled * slope(scores) * allowed).astype(jnp.bfloat16)
    result = jnp.einsum(
        "hij,jhd->ihd", score_back, split_heads(keys), preferred_element_type=jnp.float32
    ) * HEAD ** (-0.5)
    return result.reshape(queries.shape[0], -1)


def key_grads(queries, keys, values, out_back, query_pos, key_pos, length):
    scores, allowed = scores_mask(queries, keys, query_pos, key_pos, length)
    weights = attn_weights(scores, allowed)
    value_back = jnp.einsum(
        "hij,ihd->jhd", weights, split_heads(out_back), preferred_element_type=jnp.float32
    )
    pulled = jnp.einsum(
        "ihd,jhd->hij",
        split_heads(out_back),
        split_heads(values),
        preferred_element_type=jnp.float32,
    )
    score_back = (pulled * slope(scores) * allowed).astype(jnp.bfloat16)
    key_back = jnp.einsum(
        "hij,ihd->jhd", score_back, split_heads(queries), preferred_element_type=jnp.float32
    ) * HEAD ** (-0.5)
    return (key_back.reshape(keys.shape[0], -1), value_back.reshape(keys.shape[0], -1))


def blockwise(count, advance, initial):
    size = 512
    return lax.fori_loop(
        0, count // size, lambda number, running: advance(number * size, size, running), initial
    )


def local(item_table, owner, item_row, lengths, gain_in, gain_out, w_in, w_out, out_grad):
    events_here = owner.shape[1]
    owners = lax.axis_size(("seq", "table"))
    slots = max(2, 2 * events_here // owners)
    width = w_out.shape[0]
    factor = (events_here * owners) ** (-0.5)
    target = owner[0, :, 0]
    wanted = item_row[0]
    length = lengths[0]
    first = lax.axis_index("seq") * events_here
    local_pos = first + jnp.arange(events_here, dtype=jnp.int32)
    live = (local_pos < length)[:, None]
    chosen = (target[:, None] == jnp.arange(owners, dtype=jnp.int32)[None, :]).astype(jnp.int32)
    before = jnp.cumsum(chosen, axis=0) - chosen
    rank = jnp.sum(before * chosen, axis=1)
    slot = target * slots + rank
    request = jnp.full((owners * slots,), -1, jnp.int32).at[slot].set(wanted).reshape(owners, slots)
    asked = lax.all_to_all(request, ("seq", "table"), split_axis=0, concat_axis=0, tiled=True)
    found = jnp.take(item_table, jnp.maximum(asked, 0), axis=0)
    found = jnp.where((asked >= 0)[:, :, None], found, jnp.zeros_like(found))
    fetched, asked = (
        lax.all_to_all(found, ("seq", "table"), split_axis=0, concat_axis=0, tiled=True),
        asked,
    )
    embed = jnp.take(fetched.reshape(owners * slots, width), slot, axis=0)
    x_rows = embed.astype(jnp.float32)
    normed = layer_norm(x_rows, gain_in).astype(jnp.bfloat16)
    pre = jnp.dot(normed, w_in, preferred_element_type=jnp.float32)
    proj = jax.nn.silu(pre).astype(jnp.bfloat16)
    gate = proj[:, :width]
    values = proj[:, width : 2 * width]
    queries = proj[:, 2 * width : 3 * width]
    keys = proj[:, 3 * width :]
    empty = jnp.zeros((events_here, width), jnp.float32)
    key_piece = lax.all_gather(keys, "seq", axis=0, tiled=True)
    value_piece = lax.all_gather(values, "seq", axis=0, tiled=True)

    def advance(offset, size, running):
        key_block = lax.dynamic_slice_in_dim(key_piece, offset, size, 0)
        value_block = lax.dynamic_slice_in_dim(value_piece, offset, size, 0)
        key_pos = offset + jnp.arange(size, dtype=jnp.int32)
        return running + attend(queries, key_block, value_block, local_pos, key_pos, length)

    mixed = blockwise(key_piece.shape[0], advance, empty)

    def post(mixed_in, gate_in):
        return layer_norm(mixed_in, gain_out) * gate_in

    joined_full, pull_post = jax.vjp(post, mixed, gate.astype(jnp.float32))
    joined = joined_full.astype(jnp.bfloat16)
    output = jnp.dot(joined, w_out, preferred_element_type=jnp.float32) + x_rows
    hidden = (output * live.astype(jnp.float32)).astype(jnp.bfloat16)
    upstream = out_grad[0] * live.astype(jnp.bfloat16)
    joined_grad = jnp.dot(upstream, w_out.T, preferred_element_type=jnp.float32)
    mixed_full, gate_back = pull_post(joined_grad)
    mixed_back = mixed_full.astype(jnp.bfloat16)
    query_key_piece = lax.all_gather(keys, "seq", axis=0, tiled=True)
    query_value_piece = lax.all_gather(values, "seq", axis=0, tiled=True)

    def query_advance(offset, size, running):
        key_block = lax.dynamic_slice_in_dim(query_key_piece, offset, size, 0)
        value_block = lax.dynamic_slice_in_dim(query_value_piece, offset, size, 0)
        key_pos = offset + jnp.arange(size, dtype=jnp.int32)
        return running + query_grad(
            queries, key_block, value_block, mixed_back, local_pos, key_pos, length
        )

    query_back = blockwise(query_key_piece.shape[0], query_advance, empty)
    query_piece = lax.all_gather(queries, "seq", axis=0, tiled=True)
    back_piece = lax.all_gather(mixed_back, "seq", axis=0, tiled=True)

    def advance(offset, size, running):
        query_block = lax.dynamic_slice_in_dim(query_piece, offset, size, 0)
        back_block = lax.dynamic_slice_in_dim(back_piece, offset, size, 0)
        query_pos = offset + jnp.arange(size, dtype=jnp.int32)
        key_part, value_part = key_grads(
            query_block, keys, values, back_block, query_pos, local_pos, length
        )
        return (running[0] + key_part, running[1] + value_part)

    key_back, value_back = blockwise(query_piece.shape[0], advance, (empty, empty))
    proj_back = jnp.concatenate([gate_back, value_back, query_back, key_back], axis=1)
    pre_back = (proj_back * slope(pre)).astype(jnp.bfloat16)
    normed_back = jnp.dot(pre_back, w_in.T, preferred_element_type=jnp.float32)
    _, pull_in = jax.vjp(lambda rows: layer_norm(rows, gain_in), x_rows)
    embed_grad = pull_in(normed_back)[0] + upstream.astype(jnp.float32)
    outgoing = (
        jnp.zeros((owners * slots, width), jnp.float32)
        .at[slot]
        .set(embed_grad)
        .reshape(owners, slots, width)
    )
    incoming = lax.all_to_all(
        outgoing.astype(jnp.bfloat16), ("seq", "table"), split_axis=0, concat_axis=0, tiled=True
    ).astype(outgoing.dtype)
    table_grad = (
        jnp.zeros((item_table.shape[0], width), jnp.float32)
        .at[jnp.maximum(asked, 0).reshape(-1)]
        .add(incoming.reshape(-1, width))
    )
    in_term = jnp.dot(normed.T, pre_back, preferred_element_type=jnp.float32) * factor
    out_term = jnp.dot(joined.T, upstream, preferred_element_type=jnp.float32) * factor
    w_in_grad, w_out_grad = lax.psum((in_term, out_term), ("seq", "table"))
    return (hidden[None], table_grad, w_in_grad, w_out_grad)


def solution(mesh):
    placed = (
        P(("seq", "table"), None),
        P("table", "seq", None),
        P("table", "seq"),
        P("table"),
        P(),
        P(),
        P(),
        P(),
        P("table", "seq", None),
    )
    return jax.shard_map(
        local,
        mesh=mesh,
        in_specs=placed,
        out_specs=(P("table", "seq", None), P(("seq", "table"), None), P(), P()),
        check_vma=False,
    )
```

profile of v0, /device:TPU:1, one launch (start us, length us, event | category | flops | bytes accessed | tf_op | source)
XLA Modules:
  0.0 803.5 jit_solution(11599859296792993107)
XLA Ops:
  12.7 20.9 %all_to_all.19 = s32[128,1,8]{2,1,0:T(1,128)S(1)} all-to-all(s32[128,1,8]{2,1,0:T(1,128)S(1)} %bitcast.258), channel_id=1, replica_groups=mesh['seq'=8,'table'=16] {'seq','table'}, dimensions={0} | all-to-all | bytes 8192 | tf_op jit(solution)/shard_map/all_to_all | solution.py:109
  34.8 5.8 gather_fusion
  46.5 19.0 %all-to-all-done.1 = bf16[128,8,512]{2,1,0:T(8,128)(2,1)S(1)} async-done(((bf16[128,8,512]{2,1,0:T(8,128)(2,1)}), bf16[128,8,512]{2,1,0:T(8,128)(2,1)S(1)}, u32[]{:S(2)}, u32[]{:S(2)}) %all-to-all-start.1) | async-done | bytes 1048608 | tf_op jit(solution)/shard_map/all_to_all | solution.py:113
  80.6 47.3 %all-gather.5.cloned.1.call-done = bf16[4096,512]{1,0:T(8,128)(2,1)} async-done(((bf16[512,512]{1,0:T(8,128)(2,1)}), bf16[4096,512]{1,0:T(8,128)(2,1)}) %all-gather.5.cloned.1.call-update) | async-done | bytes 4194320 | tf_op jit(solution)/shard_map/all_gather | solution.py:127
  128.0 6.3 copy.97
  134.3 46.7 %all-gather.7.cloned.1.call-done = bf16[4096,512]{1,0:T(8,128)(2,1)} async-done(((bf16[512,512]{1,0:T(8,128)(2,1)}), bf16[4096,512]{1,0:T(8,128)(2,1)}) %all-gather.7.cloned.1.call-update) | async-done | bytes 4194320 | tf_op jit(solution)/shard_map/all_gather | solution.py:126
  181.0 6.5 copy.98
  187.4 82.7 %while.44 = (s32[]{:T(128)}, f32[512,512]{0,1:T(8,128)S(1)}, bf16[4096,512]{0,1:T(8,128)(2,1)}, bf16[4096,512]{0,1:T(8,128)(2,1)}, bf16[512,512]{1,0:T(8,128)(2,...) while((s32[]{:T(128)}, f32[512,512]{0,1:T(8,128)S(1)}, ...), condition=%wide.region_7.8_spmd.clone, body=%wide.region_6.7_spmd.clone.sunk | while | flops 545786880 | bytes 9971901 | solution.py:87
  278.2 124.3 %while.46 = (s32[]{:T(128)}, f32[512,512]{0,1:T(8,128)}, bf16[4096,512]{0,1:T(8,128)(2,1)}, bf16[4096,512]{0,1:T(8,128)(2,1)}, bf16[512,512]{1,0:T(8,128)(2,1)},...) while((s32[]{:T(128)}, f32[512,512]{0,1:T(8,128)}, ...), condition=%wide.region_15.16_spmd.clone, body=%wide.region_14.15_spmd.clone.sunk | while | flops 818678784 | bytes 19409092 | solution.py:87
  284.9 6.3 fusion.169
  300.3 6.2 fusion.169
  316.0 6.1 fusion.169
  331.6 6.1 fusion.169
  347.1 6.1 fusion.169
  362.6 6.1 fusion.169
  378.1 6.1 fusion.169
  393.7 6.1 fusion.169
  407.9 204.7 %while.45 = (s32[]{:T(128)}, f32[512,512]{0,1:T(8,128)}, f32[512,512]{0,1:T(8,128)}, bf16[4096,512]{1,0:T(8,128)(2,1)}, bf16[4096,512]{1,0:T(8,128)(2,1)}, /*ind...) while((s32[]{:T(128)}, f32[512,512]{0,1:T(8,128)}, ...), condition=%wide.region_13.14_spmd.clone, body=%wide.region_12.13_spmd.clone.sunk | while | flops 1094978560 | bytes 39856396 | solution.py:87
  417.7 6.1 fusion.160
  423.8 5.1 fusion.159
  443.0 6.1 fusion.160
  468.6 6.1 fusion.160
  494.3 6.1 fusion.160
  500.4 5.1 fusion.159
  519.9 6.1 fusion.160
  545.5 6.1 fusion.160
  571.2 6.1 fusion.160
  596.8 6.1 fusion.160
  639.3 7.6 all-to-all-start.2
  649.2 17.6 %all-to-all-done.2 = bf16[128,8,512]{2,1,0:T(8,128)(2,1)} async-done(((bf16[128,8,512]{2,1,0:T(8,128)(2,1)}), bf16[128,8,512]{2,1,0:T(8,128)(2,1)}, u32[]{:S(2)}, u32[]{:S(2)}) %all-to-all-start.2) | async-done | bytes 1048608 | tf_op jit(solution)/shard_map/all_to_all | solution.py:184
  666.9 9.4 %scatter_custom_fusion.2 = f32[2048,512]{1,0:T(8,128)} fusion(s32[1024]{0:T(1024)} %copy-done.18, f32[]{:T(128)} %constant.190.clone.1, bf16[128,8,512]{2,1,0:T(8,128)(2,1)} %all-to-all-done.2), kind=kCustom, calls=%fused_computation.84 | custom fusion | flops 1048576 | bytes 5243392 | tf_op jit(solution)/shard_map/scatter-add | solution.py:190
  676.3 114.9 %all-reduce.3.cloned.1.call-done = (f32[512,2048]{1,0:T(8,128)}, f32[512,512]{1,0:T(8,128)}) async-done(((f32[512,2048]{1,0:T(8,128)}, f32[512,512]{1,0:T(8,128)}), (f32[512,2048]{1,0:T(8,128)}, f32[512,512]{1,0:T(8,128)})) %all-reduce.3.cloned.1.call-update) | async-done | bytes 5242896 | tf_op jit(solution)/shard_map/psum | solution.py:194
  (340 shorter events, 377.5 us)
Async XLA Ops:
  7.2 64.3 %copy-start = (bf16[512,2048]{1,0:T(8,128)(2,1)S(1)}, bf16[512,2048]{1,0:T(8,128)(2,1)}, u32[]{:S(2)}) copy-start(bf16[512,2048]{1,0:T(8,128)(2,1)} %param.21) | copy-start | bytes 6291460
  10.0 36.4 %copy-start.21 = (s32[512,1]{0,1:T(1,128)}, s32[512,1]{0,1:T(1,128)S(1)}, u32[]{:S(2)}) copy-start(s32[512,1]{0,1:T(1,128)S(1)} %compare_select_fusion) | copy-start | bytes 6148
  40.6 5.9 copy-start.13
  41.9 29.6 %copy-start.23 = (f32[512]{0:T(512)S(1)}, f32[512]{0:T(512)}, u32[]{:S(2)}) copy-start(f32[512]{0:T(512)} %param.19) | copy-start | bytes 6148
  41.9 23.7 %all-to-all-start.1 = ((bf16[128,8,512]{2,1,0:T(8,128)(2,1)}), bf16[128,8,512]{2,1,0:T(8,128)(2,1)S(1)}, u32[]{:S(2)}, u32[]{:S(2)}) async-start(bf16[128,8,512]{2,1,0:T(8,128)(2,1)} %fusion.69), calls=%async_computation.1 | async-start | bytes 2097152 | tf_op jit(solution)/shard_map/all_to_all | solution.py:113
  46.4 81.6 %all-gather.5.cloned.1.call-start = ((), (), s32[]{:S(2)}) async-start(), calls=%async_computation.3 | async-start | bytes 4718592 | tf_op jit(solution)/shard_map/all_gather | solution.py:127
  46.5 29.8 %copy-start.19 = (pred[512]{0:T(512)(128)(4,1)}, pred[512]{0:T(512)(128)(4,1)S(1)}, u32[]{:S(2)}) copy-start(pred[512]{0:T(512)(128)(4,1)S(1)} %compare_and_fusion) | copy-start | bytes 1540
  69.5 6.8 copy-start.11
  71.5 4.8 copy-start.14
  78.9 102.1 %all-gather.7.cloned.1.call-start = ((), (), s32[]{:S(2)}) async-start(), calls=%async_computation.4 | async-start | bytes 4718592 | tf_op jit(solution)/shard_map/all_gather | solution.py:126
  79.6 328.3 %all-gather.9.cloned.1.call-start = ((), (), s32[]{:S(2)}) async-start(), calls=%async_computation.5 | async-start | bytes 4718592 | tf_op jit(solution)/shard_map/all_gather | solution.py:160
  80.4 327.5 %all-gather.11.cloned.1.call-start = ((), (), s32[]{:S(2)}) async-start(), calls=%async_computation.6 | async-start | bytes 4718592 | tf_op jit(solution)/shard_map/all_gather | solution.py:161
  187.4 84.1 %copy-start.22 = (f32[512]{0:T(512)S(1)}, f32[512]{0:T(512)}, u32[]{:S(2)}) copy-start(f32[512]{0:T(512)} %param.20) | copy-start | bytes 6148
  274.0 4.2 copy-start.3
  277.9 513.3 %all-reduce.3.cloned.1.call-start = ((), (), s32[]{:S(2)}) async-start(), calls=%async_computation.7 | async-start | bytes 10485760 | tf_op jit(solution)/shard_map/psum | solution.py:194
  423.8 5.1 copy-start.1
  449.1 5.1 copy-start.1
  474.7 5.1 copy-start.1
  500.4 5.1 copy-start.1
  526.0 5.1 copy-start.1
  551.6 5.1 copy-start.1
  577.3 5.1 copy-start.1
  602.9 5.1 copy-start.1
  617.7 5.9 copy-start.4
  617.7 5.9 copy-start.12
  617.7 5.9 copy-start.15
  617.7 5.9 copy-start.20
  617.7 5.9 copy-start.24
  627.1 3.0 copy-start.17
  631.6 15.3 %copy-start.10 = (bf16[512,512]{1,0:T(8,128)(2,1)S(1)}, bf16[512,512]{1,0:T(8,128)(2,1)}, u32[]{:S(2)}) copy-start(bf16[512,512]{1,0:T(8,128)(2,1)} %get-tuple-element.672) | copy-start | bytes 1572868
  639.3 27.6 %all-to-all-start.2 = ((bf16[128,8,512]{2,1,0:T(8,128)(2,1)}), bf16[128,8,512]{2,1,0:T(8,128)(2,1)}, u32[]{:S(2)}, u32[]{:S(2)}) async-start(bf16[128,8,512]{2,1,0:T(8,128)(2,1)} %convert_bitcast_fusion), calls=%async_computation.2 | async-start | bytes 2097152 | tf_op jit(solution)/shard_map/all_to_all | solution.py:184
  791.2 4.8 copy-start.9
  (14 other events, 15.2 us)
Sparse Core Ops, SparseCore 0:
  79.0 48.9 all-gather.4
  129.6 51.3 all-gather.6
  182.6 51.3 all-gather.8
  278.1 51.4 all-gather.10
  627.2 163.9 all-reduce.2
where the time goes:
time: 807 us; the launch traced here: 803 us
  waiting for transfers between devices  246 us (30%)
  matrix products  246 us (30%)
  other arithmetic  145 us (18%)
  local copies, waits for them, and re-layouts  116 us (14%)
  blocking collectives  20.9 us (3%)
  between operations  14.8 us (2%)
  starting transfers between devices  12.8 us (2%)
    psum x1, waiting for transfers between devices, local(): w_in_grad, w_out_grad = lax.psum((in_term, out_term), ('seq', 'table'))  115 us
    dot_general x16, matrix products, scores_mask(): jnp.einsum('ihd,jhd->hij', split_heads(queries), split_heads(keys), prefe...  52 us
    dot_general x8, matrix products, query_grad(): jnp.einsum('hij,jhd->ihd', score_back, split_heads(keys), preferred_eleme...  49.1 us
    dot_general x8, matrix products, key_grads(): jnp.einsum('hij,ihd->jhd', score_back, split_heads(queries), preferred_el...  48.9 us
    all_gather x1, waiting for transfers between devices, local(): value_piece = lax.all_gather(values, 'seq', axis=0, tiled=True)  47.3 us
    all_gather x1, waiting for transfers between devices, local(): key_piece = lax.all_gather(keys, 'seq', axis=0, tiled=True)  46.7 us
    dot_general x8, matrix products, key_grads(): jnp.einsum('hij,ihd->jhd', weights, split_heads(out_back), preferred_elem...  41.1 us
    dot_general x8, matrix products, attend(): jnp.einsum('hij,jhd->ihd', weights, split_heads(values), preferred_elemen...  36.5 us
  transfers between devices with their start and end apart: 7, of which 5 were waited for; matrix products, arithmetic and copies ran while one was open for 32% of the time, Pallas kernels for 0%

commit v1 on v0

v1 whole, which is shorter than its diff:
```python
import functools

import jax
import jax.numpy as jnp
from jax import lax
from jax.experimental import pallas as pl
from jax.experimental.pallas import tpu as pltpu
from jax.sharding import PartitionSpec as P

HEADS = 4
HEAD = 128
TOK = 512
WIDTH = 512
TILE = 128
SCALE = HEAD ** (-0.5)
EPS = 1e-05
MESH = pl.DeviceIdType.MESH
BF = jnp.bfloat16
F32 = jnp.float32


def dot(a, b, ca=1, cb=0):
    return lax.dot_general(a, b, (((ca,), (cb,)), ((), ())), preferred_element_type=F32)


def landed(ref, sem):
    pltpu.make_async_copy(ref, ref, sem).wait()


def layer_kernel(
    factor,
    len_ref, x_ref, og_ref, gin_ref, gout_ref, w_in_ref, w_out_ref,
    hidden_ref, egrad_ref, interm_ref, outterm_ref,
    normed, normed_t, slope, gate, upstream, joined, jgrad, nback, pback,
    q_out, kv_out, q_in, kv_in, mix_out, mix_in, dm_out, dm_in,
    dq_acc, dkv_acc, part_out, part_in, dq_out, dkv_out, dq_in, dkv_in, m_acc,
    q_send, q_recv, kv_send, kv_recv, fwd_send, mix_send, mix_recv, dm_send, dm_recv,
    part_send, part_recv, dq_send, dq_recv, dkv_send, dkv_recv,
):
    s = lax.axis_index("seq")
    t = lax.axis_index("table")
    core = lax.rem(t, 2)
    base = t - core
    head = lax.rem(s, HEADS)
    user_core = s // HEADS
    sibling = base + 1 - core
    part_of_s = lax.rem((s + 1) // 2, 2)
    slot_of_s = s // 2

    barrier = pltpu.get_barrier_semaphore()
    me = s * 2 + core

    def greet(d, carry):
        other = lax.rem(me + d, 16)
        pl.semaphore_signal(
            barrier, inc=1, device_id=(other // 2, base + lax.rem(other, 2)), device_id_type=MESH
        )
        return carry

    lax.fori_loop(1, 16, greet, 0)
    pl.semaphore_wait(barrier, 15)

    def push(src, dst, send, recv, to_s, to_t):
        mine = jnp.logical_and(to_s == s, to_t == t)

        @pl.when(mine)
        def _():
            pltpu.make_async_copy(src, dst, recv).start()

        @pl.when(jnp.logical_not(mine))
        def _():
            pltpu.make_async_remote_copy(
                src_ref=src, dst_ref=dst, send_sem=send, recv_sem=recv,
                device_id=(to_s, to_t), device_id_type=MESH,
            ).start()

    def left(src, send, to_s, to_t):
        @pl.when(jnp.logical_not(jnp.logical_and(to_s == s, to_t == t)))
        def _():
            landed(src, send)

    def worker(h):
        return core * HEADS + h, base + part_of_s

    def mine_of(k):
        return 2 * k + lax.rem(k + core, 2)

    def other_of(k):
        return 2 * k + lax.rem(k + core + 1, 2)

    length = len_ref[0]

    def live_rows(start, count):
        pos = s * TOK + start + lax.broadcasted_iota(jnp.int32, (count, 1), 0)
        return (pos < length).astype(F32)

    def norm_tile(r, carry):
        rows = pl.ds(pl.multiple_of(r * TILE, TILE), TILE)
        x = x_ref[rows, :].astype(F32)
        mean = jnp.mean(x, -1, keepdims=True)
        cent = x - mean
        var = jnp.mean(cent * cent, -1, keepdims=True)
        normed[rows, :] = (cent * lax.rsqrt(var + EPS) * gin_ref[...]).astype(BF)
        return carry

    lax.fori_loop(0, TOK // TILE, norm_tile, 0)

    live = live_rows(0, TOK)

    def project(first, columns):
        pre = dot(normed[...], w_in_ref[:, pl.ds(first, columns)])
        half = 0.5 * pre
        th = jnp.tanh(half)
        slope[:, pl.ds(first, columns)] = 0.5 * (1.0 + th) * (1.0 + half - half * th)
        return half + half * th

    for h in range(HEADS):
        kv_out[h, :, :HEAD] = project(3 * WIDTH + h * HEAD, HEAD).astype(BF)
        kv_out[h, :, HEAD:] = (project(WIDTH + h * HEAD, HEAD) * live).astype(BF)
        to = worker(h)
        push(kv_out.at[h], kv_in.at[s], kv_send.at[h], kv_recv.at[s], *to)
        q_out[h] = project(2 * WIDTH + h * HEAD, HEAD).astype(BF)
        push(q_out.at[h], q_in.at[slot_of_s], q_send.at[h], q_recv.at[slot_of_s], *to)

    gate[:, :256] = project(0, 256).astype(BF)
    gate[:, 256:] = project(256, 256).astype(BF)
    upstream[...] = (og_ref[...].astype(F32) * live).astype(BF)
    jgrad[...] = dot(upstream[...], w_out_ref[...], 1, 1)
    normed_t[...] = normed[...].T
    dq_acc[...] = jnp.zeros_like(dq_acc)
    dkv_acc[...] = jnp.zeros_like(dkv_acc)

    def take(k):
        d = mine_of(k)
        landed(kv_in.at[d], kv_recv.at[d])
        pltpu.make_async_remote_copy(
            src_ref=kv_in.at[d], dst_ref=kv_in.at[d], send_sem=fwd_send.at[k], recv_sem=kv_recv.at[d],
            device_id=(s, sibling), device_id_type=MESH,
        ).start()

    row = lax.broadcasted_iota(jnp.int32, (TOK, TOK), 0)
    col = lax.broadcasted_iota(jnp.int32, (TOK, TOK), 1)

    def forward_pair(k, j, diagonal):
        half = dot(q_in[k], kv_in[j, :, :HEAD], 1, 1) * (0.5 * SCALE)
        w = half + half * jnp.tanh(half)
        if diagonal:
            w = jnp.where(col <= row, w, 0.0)
        return dot(w.astype(BF), kv_in[j, :, HEAD:])

    take(0)

    def forward(k, carry):
        i = mine_of(k)

        @pl.when(k < 3)
        def _():
            take(k + 1)

        landed(q_in.at[k], q_recv.at[k])
        o = other_of(k)
        landed(kv_in.at[o], kv_recv.at[o])
        m_acc[...] = forward_pair(k, i, True)

        def inner(j, c):
            m_acc[...] += forward_pair(k, j, False)
            return c

        lax.fori_loop(0, i, inner, 0)
        mix_out[k] = m_acc[...].astype(BF)
        push(mix_out.at[k], mix_in.at[head], mix_send.at[k], mix_recv.at[head], i, base + user_core)
        return carry

    lax.fori_loop(0, 4, forward, 0)

    for h in range(HEADS):
        landed(mix_in.at[h], mix_recv.at[h])

    def post_tile(r, carry):
        start = pl.multiple_of(r * TILE, TILE)
        rows = pl.ds(start, TILE)
        alive = live_rows(start, TILE)
        m = jnp.concatenate([mix_in[h, rows, :] for h in range(HEADS)], axis=1).astype(F32) * alive
        mean = jnp.mean(m, -1, keepdims=True)
        cent = m - mean
        var = jnp.mean(cent * cent, -1, keepdims=True)
        rstd = lax.rsqrt(var + EPS)
        n = cent * rstd
        ng = n * gout_ref[...]
        g = gate[rows, :].astype(F32)
        jg = jgrad[rows, :]
        joined[rows, :] = (ng * g).astype(BF)
        pback[rows, :WIDTH] = (jg * ng * slope[rows, :WIDTH]).astype(BF)
        dn = jg * g * gout_ref[...]
        dm = rstd * (dn - jnp.mean(dn, -1, keepdims=True) - n * jnp.mean(dn * n, -1, keepdims=True))
        dm = (dm * alive).astype(BF)
        for h in range(HEADS):
            dm_out[h, rows, :] = dm[:, h * HEAD : (h + 1) * HEAD]
        return carry

    lax.fori_loop(0, TOK // TILE, post_tile, 0)
    for h in range(HEADS):
        push(dm_out.at[h], dm_in.at[slot_of_s], dm_send.at[h], dm_recv.at[slot_of_s], *worker(h))

    hidden_ref[...] = ((dot(joined[...], w_out_ref[...]) + x_ref[...].astype(F32)) * live).astype(BF)
    outterm_ref[...] = dot(joined[...], upstream[...], 0, 0) * factor
    interm_ref[:, :WIDTH] = dot(normed_t[...], pback[:, :WIDTH]) * factor
    nback[...] = dot(pback[:, :WIDTH], w_in_ref[:, :WIDTH], 1, 1)

    for k in range(4):
        landed(dm_in.at[k], dm_recv.at[k])

    def backward_pair(k, j, diagonal):
        q, dm = q_in[k], dm_in[k]
        half = dot(kv_in[j, :, :HEAD], q, 1, 1) * (0.5 * SCALE)
        th = jnp.tanh(half)
        ht = half * th
        w = half + ht
        sb = dot(kv_in[j, :, HEAD:], dm, 1, 1) * ((0.5 + 0.5 * th) * (1.0 + half - ht))
        if diagonal:
            w = jnp.where(row <= col, w, 0.0)
            sb = jnp.where(row <= col, sb, 0.0)
        sb = sb.astype(BF)
        dkv_acc[j, :, HEAD:] += dot(w.astype(BF), dm)
        dkv_acc[j, :, :HEAD] += dot(sb, q)
        dq_acc[k] += dot(sb, kv_in[j, :, :HEAD], 0, 0)

    def finish(m):
        d = mine_of(m)
        landed(part_in.at[m], part_recv.at[m])
        total = dkv_acc[d] + part_in[m].astype(F32)
        dkv_out[m, :, :HEAD] = (total[:, :HEAD] * SCALE).astype(BF)
        dkv_out[m, :, HEAD:] = total[:, HEAD:].astype(BF)
        push(dkv_out.at[m], dkv_in.at[head], dkv_send.at[m], dkv_recv.at[head], d, base + user_core)

    def backward(m, carry):
        i = mine_of(m)

        def one(jj, c):
            j = 2 * m + jj

            @pl.when(i == j)
            def _():
                backward_pair(m, j, True)

            def inner(k, cc):
                backward_pair(k, j, False)
                return cc

            lax.fori_loop(jnp.where(i > j, m, m + 1), 4, inner, 0)
            return c

        lax.fori_loop(0, 2, one, 0)
        part_out[m] = dkv_acc[other_of(m)].astype(BF)
        pltpu.make_async_remote_copy(
            src_ref=part_out.at[m], dst_ref=part_in.at[m], send_sem=part_send.at[m], recv_sem=part_recv.at[m],
            device_id=(s, sibling), device_id_type=MESH,
        ).start()
        dq_out[m] = (dq_acc[m] * SCALE).astype(BF)
        push(dq_out.at[m], dq_in.at[head], dq_send.at[m], dq_recv.at[head], i, base + user_core)

        @pl.when(m > 0)
        def _():
            finish(m - 1)

        return carry

    lax.fori_loop(0, 4, backward, 0)
    finish(3)

    for h in range(HEADS):
        landed(dq_in.at[h], dq_recv.at[h])
        landed(dkv_in.at[h], dkv_recv.at[h])

    def back_tile(r, carry):
        start = pl.multiple_of(r * TILE, TILE)
        rows = pl.ds(start, TILE)
        alive = live_rows(start, TILE)
        for h in range(HEADS):
            for first, piece in (
                (WIDTH, dkv_in[h, rows, HEAD:].astype(F32) * alive),
                (2 * WIDTH, dq_in[h, rows, :].astype(F32)),
                (3 * WIDTH, dkv_in[h, rows, :HEAD].astype(F32)),
            ):
                c = first + h * HEAD
                pback[rows, c : c + HEAD] = (piece * slope[rows, c : c + HEAD]).astype(BF)
        nb = nback[rows, :] + dot(pback[rows, WIDTH:], w_in_ref[:, WIDTH:], 1, 1)
        x = x_ref[rows, :].astype(F32)
        mean = jnp.mean(x, -1, keepdims=True)
        cent = x - mean
        var = jnp.mean(cent * cent, -1, keepdims=True)
        rstd = lax.rsqrt(var + EPS)
        n = cent * rstd
        dn = nb * gin_ref[...]
        dx = rstd * (dn - jnp.mean(dn, -1, keepdims=True) - n * jnp.mean(dn * n, -1, keepdims=True))
        egrad_ref[rows, :] = (dx + upstream[rows, :].astype(F32)).astype(BF)
        return carry

    lax.fori_loop(0, TOK // TILE, back_tile, 0)

    def in_columns(c, carry):
        cols = pl.ds(pl.multiple_of(c * 256, 256), 256)
        interm_ref[:, cols] = dot(normed_t[...], pback[:, cols]) * factor
        return carry

    lax.fori_loop(2, 8, in_columns, 0)

    for h in range(HEADS):
        to = worker(h)
        left(kv_out.at[h], kv_send.at[h], *to)
        left(q_out.at[h], q_send.at[h], *to)
        left(dm_out.at[h], dm_send.at[h], *to)
        landed(kv_in.at[mine_of(h)], fwd_send.at[h])
        landed(part_out.at[h], part_send.at[h])
        back = (mine_of(h), base + user_core)
        left(mix_out.at[h], mix_send.at[h], *back)
        left(dq_out.at[h], dq_send.at[h], *back)
        left(dkv_out.at[h], dkv_send.at[h], *back)


def layer(length, embed, out_grad, gain_in, gain_out, w_in, w_out, factor):
    vm = pl.BlockSpec(memory_space=pltpu.VMEM)
    dma = pltpu.SemaphoreType.DMA

    def buf(*shape, dtype=BF):
        return pltpu.VMEM(shape, dtype)

    blocks = [
        buf(TOK, WIDTH), buf(WIDTH, TOK), buf(TOK, 4 * WIDTH, dtype=F32), buf(TOK, WIDTH), buf(TOK, WIDTH),
        buf(TOK, WIDTH), buf(TOK, WIDTH, dtype=F32), buf(TOK, WIDTH, dtype=F32), buf(TOK, 4 * WIDTH),
        buf(4, TOK, HEAD), buf(4, TOK, 2 * HEAD), buf(4, TOK, HEAD), buf(8, TOK, 2 * HEAD),
        buf(4, TOK, HEAD), buf(4, TOK, HEAD), buf(4, TOK, HEAD), buf(4, TOK, HEAD),
        buf(4, TOK, HEAD, dtype=F32), buf(8, TOK, 2 * HEAD, dtype=F32),
        buf(4, TOK, 2 * HEAD), buf(4, TOK, 2 * HEAD), buf(4, TOK, HEAD), buf(4, TOK, 2 * HEAD),
        buf(4, TOK, HEAD), buf(4, TOK, 2 * HEAD), buf(TOK, HEAD, dtype=F32),
    ]
    sems = [dma((n,)) for n in (4, 4, 4, 8, 4, 4, 4, 4, 4, 4, 4, 4, 4, 4, 4)]
    return pl.pallas_call(
        functools.partial(layer_kernel, factor),
        out_shape=(
            jax.ShapeDtypeStruct((TOK, WIDTH), BF),
            jax.ShapeDtypeStruct((TOK, WIDTH), BF),
            jax.ShapeDtypeStruct((WIDTH, 4 * WIDTH), F32),
            jax.ShapeDtypeStruct((WIDTH, WIDTH), F32),
        ),
        in_specs=[pl.BlockSpec(memory_space=pltpu.SMEM)] + [vm] * 6,
        out_specs=(vm,) * 4,
        scratch_shapes=blocks + sems,
        compiler_params=pltpu.CompilerParams(
            collective_id=0, has_side_effects=True, vmem_limit_bytes=56 * 1024 * 1024
        ),
        cost_estimate=pl.CostEstimate(flops=14 * 10**9, bytes_accessed=12 * 2**20, transcendentals=10**7),
    )(length, embed, out_grad, gain_in.reshape(1, -1), gain_out.reshape(1, -1), w_in, w_out)


def local(item_table, owner, item_row, lengths, gain_in, gain_out, w_in, w_out, out_grad):
    events_here = owner.shape[1]
    owners = lax.axis_size(("seq", "table"))
    slots = max(2, 2 * events_here // owners)
    width = w_out.shape[0]
    factor = (events_here * owners) ** (-0.5)
    target = owner[0, :, 0]
    wanted = item_row[0]
    chosen = (target[:, None] == jnp.arange(owners, dtype=jnp.int32)[None, :]).astype(jnp.int32)
    before = jnp.cumsum(chosen, axis=0) - chosen
    rank = jnp.sum(before * chosen, axis=1)
    slot = target * slots + rank
    request = jnp.full((owners * slots,), -1, jnp.int32).at[slot].set(wanted).reshape(owners, slots)
    asked = lax.all_to_all(request, ("seq", "table"), split_axis=0, concat_axis=0, tiled=True)
    found = jnp.take(item_table, jnp.maximum(asked, 0), axis=0)
    found = jnp.where((asked >= 0)[:, :, None], found, jnp.zeros_like(found))
    fetched = lax.all_to_all(found, ("seq", "table"), split_axis=0, concat_axis=0, tiled=True)
    embed = jnp.take(fetched.reshape(owners * slots, width), slot, axis=0)
    hidden, embed_grad, in_term, out_term = layer(
        lengths, embed, out_grad[0], gain_in, gain_out, w_in, w_out, factor
    )
    outgoing = jnp.zeros((owners * slots, width), jnp.bfloat16).at[slot].set(embed_grad).reshape(owners, slots, width)
    incoming = lax.all_to_all(outgoing, ("seq", "table"), split_axis=0, concat_axis=0, tiled=True)
    table_grad = (
        jnp.zeros((item_table.shape[0], width), jnp.float32)
        .at[jnp.maximum(asked, 0).reshape(-1)]
        .add(incoming.reshape(-1, width).astype(jnp.float32))
    )
    w_in_grad, w_out_grad = lax.psum((in_term, out_term), ("seq", "table"))
    return (hidden[None], table_grad, w_in_grad, w_out_grad)


def solution(mesh):
    placed = (
        P(("seq", "table"), None),
        P("table", "seq", None),
        P("table", "seq"),
        P("table"),
        P(),
        P(),
        P(),
        P(),
        P("table", "seq", None),
    )
    return jax.shard_map(
        local,
        mesh=mesh,
        in_specs=placed,
        out_specs=(P("table", "seq", None), P(("seq", "table"), None), P(), P()),
        check_vma=False,
    )
```

time: 807 us -> 345 us (0.43)
  matrix products: 246 us -> 0 us
  other arithmetic: 145 us -> 14.1 us
  local copies, waits for them, and re-layouts: 116 us -> 22.3 us
  Pallas kernels: 0 us -> 88.2 us
  waiting for transfers between devices: 246 us -> 163 us
  starting transfers between devices: 12.8 us -> 22.1 us
    dot_general x54 -> x0, matrix products: 246 us -> none  [the longest x16 52 us: scores_mask(): jnp.einsum('ihd,jhd->hij', split_heads(queries), split_heads(keys), prefe...]
    all_gather x4 -> x0, waiting for transfers between devices: 94 us -> none  [the longest x1 47.3 us: local(): value_piece = lax.all_gather(values, 'seq', axis=0, tiled=True)]
    pallas_call x0 -> x1, Pallas kernels: none -> 88.2 us  [layer(): pl.pallas_call(functools.partial(layer_kernel, factor), out_shape=(jax.Sh...]
    add x56 -> x0, other arithmetic: 62.9 us -> none  [the longest x8 28.3 us: advance(): return (running[0] + key_part, running[1] + value_part)]
    dynamic_slice x48 -> x0, local copies, waits for them, and re-layouts: 62.2 us -> none  [the longest x8 18.3 us: advance(): key_block = lax.dynamic_slice_in_dim(key_piece, offset, size, 0)]
    convert_element_type x29 -> x0, other arithmetic: 37.9 us -> none  [the longest x24 29.7 us: scores_mask(): return (scores, allowed.astype(jnp.float32)[None])]
    lt x32 -> x0, other arithmetic: 20.9 us -> none  [the longest x24 15.6 us: scores_mask(): query_pos[:, None] < length]
    while x36 -> x0, local copies, waits for them, and re-layouts: 16.9 us -> none  [the longest x4 8.93 us: blockwise(): lax.fori_loop(0, count // size, lambda number, running: advance(number *...]
  transfers between devices with their start and end apart: 7 -> 3, of which waited for: 5 -> 3; matrix products, arithmetic and copies ran while one was open for 32% -> 4% of each run, Pallas kernels for 0% -> 0%
where the time goes in v1:
time: 345 us
  waiting for transfers between devices  163 us (47%)
  Pallas kernels  88.2 us (26%)
  local copies, waits for them, and re-layouts  22.3 us (6%)
  starting transfers between devices  22.1 us (6%)
  blocking collectives  20.9 us (6%)
  between operations  14.8 us (4%)
  other arithmetic  14.1 us (4%)
    psum x1, waiting for transfers between devices, local(): w_in_grad, w_out_grad = lax.psum((in_term, out_term), ('seq', 'table'))  124 us
    pallas_call x1, Pallas kernels, layer(): pl.pallas_call(functools.partial(layer_kernel, factor), out_shape=(jax.Sh...  88.2 us
    all_to_all x1, blocking collectives, local(): lax.all_to_all(request, ('seq', 'table'), split_axis=0, concat_axis=0, ti...  20.9 us
    all_to_all x1, waiting for transfers between devices, local(): lax.all_to_all(outgoing, ('seq', 'table'), split_axis=0, concat_axis=0, t...  19.7 us
    all_to_all x1, waiting for transfers between devices, local(): lax.all_to_all(found, ('seq', 'table'), split_axis=0, concat_axis=0, tile...  18.4 us
    all_to_all x1, starting transfers between devices, local(): lax.all_to_all(outgoing, ('seq', 'table'), split_axis=0, concat_axis=0, t...  17.5 us
    scatter-add x1, other arithmetic, local(): table_grad = jnp.zeros((item_table.shape[0], width), jnp.float32).at[jnp....  8.95 us
    unnamed x10, local copies, waits for them, and re-layouts  7.65 us
  transfers between devices with their start and end apart: 3, of which 3 were waited for; matrix products, arithmetic and copies ran while one was open for 4% of the time, Pallas kernels for 0%

profile of v1, /device:TPU:1, one launch (start us, length us, event | category | flops | bytes accessed | tf_op | source)
XLA Modules:
  0.0 344.9 jit_solution(17710680080777301979)
XLA Ops:
  7.2 0.0 copy-start
  7.2 0.9 copy.19
  8.1 0.2 fusion.9
  8.4 0.9 fusion.8
  9.3 0.7 compare_select_fusion
  10.0 2.6 scatter_custom_fusion
  12.6 0.1 all_to_all.12
  12.7 20.9 %all_to_all.19 = s32[128,1,8]{2,1,0:T(1,128)S(1)} all-to-all(s32[128,1,8]{2,1,0:T(1,128)S(1)} %bitcast.51), channel_id=1, replica_groups=mesh['seq'=8,'table'=16] {'seq','table'}, dimensions={0} | all-to-all | bytes 8192 | tf_op jit(solution)/shard_map/all_to_all | solution.py:369
  33.7 0.1 copy.23
  33.8 0.1 copy.25
  34.0 0.1 copy.26
  34.1 0.1 reshape.130
  34.2 0.0 copy-done
  34.2 4.0 %gather_fusion = bf16[1024,512]{1,0:T(8,128)(2,1)S(1)} fusion(bf16[2048,512]{1,0:T(8,128)(2,1)S(1)} %copy-done, s32[1024]{0:T(1024)S(1)} %broadcast_clamp_fusion), kind=kCustom, calls=%fused_computation | custom fusion | bytes 2101248 | tf_op jit(solution)/shard_map/jit(_take)/gather | solution.py:370
  38.2 0.0 copy-start.2
  38.2 1.2 fusion.4
  39.4 4.5 %all-to-all-start.1 = ((bf16[128,8,512]{2,1,0:T(8,128)(2,1)}), bf16[128,8,512]{2,1,0:T(8,128)(2,1)S(1)}, u32[]{:S(2)}, u32[]{:S(2)}) async-start(bf16[128,8,512]{2,1,0:T(8,128)(2,1)} %fusion.4), calls=%async_computation.1 | async-start | bytes 2097152 | tf_op jit(solution)/shard_map/all_to_all | solution.py:372
  43.9 0.0 all-reduce.3.cloned.1.call-start
  44.6 0.0 copy-done.2
  44.7 18.4 %all-to-all-done.1 = bf16[128,8,512]{2,1,0:T(8,128)(2,1)S(1)} async-done(((bf16[128,8,512]{2,1,0:T(8,128)(2,1)}), bf16[128,8,512]{2,1,0:T(8,128)(2,1)S(1)}, u32[]{:S(2)}, u32[]{:S(2)}) %all-to-all-start.1) | async-done | bytes 1048608 | tf_op jit(solution)/shard_map/all_to_all | solution.py:372
  63.1 2.6 gather_fusion.1
  65.7 2.0 broadcast_select_fusion.x_ref
  67.7 88.2 %shard_map.120 = (bf16[512,512]{1,0:T(8,128)(2,1)}, bf16[512,512]{1,0:T(8,128)(2,1)}, f32[512,2048]{1,0:T(8,128)}, f32[512,512]{1,0:T(8,128)}) custom-call(s32[1]{0:T(128)S(6)} %copy.32.len_ref, bf16[512,512]{1,0:T(8,128)(2,1)} %broadcast_select_fusion.x_ref, bf16[512,512]{1,0:T(8,128)(2,1)} %bitcast.60, f32[1,512]{1,0:T(1,128)} %bitcast.62, ...), custom_call_target="tpu_custom_call" | custom-call | flops 14000000000 | bytes 12582912 | tf_op jit(solution)/shard_map/pallas_call | solution.py:338
  155.8 0.0 all-reduce.3.cloned.1.call-update
  155.9 4.0 %scatter_custom_fusion.1 = bf16[1024,512]{1,0:T(8,128)(2,1)} fusion(s32[512]{0:T(512)S(1)} %bitcast.59, bf16[512,512]{1,0:T(8,128)(2,1)} %get-tuple-element.9, bf16[]{:T(256)} %constant.49.clone.1), kind=kCustom, calls=%fused_computation.11 | custom fusion | bytes 1049088 | tf_op jit(solution)/shard_map/scatter | solution.py:377
  159.8 17.5 %all-to-all-start.2 = ((bf16[128,8,512]{2,1,0:T(8,128)(2,1)}), bf16[128,8,512]{2,1,0:T(8,128)(2,1)S(1)}, u32[]{:S(2)}, u32[]{:S(2)}) async-start(bf16[128,8,512]{2,1,0:T(8,128)(2,1)} %bitcast.18), calls=%async_computation.2 | async-start | bytes 2097152 | tf_op jit(solution)/shard_map/all_to_all | solution.py:378
  177.3 19.7 %all-to-all-done.2 = bf16[128,8,512]{2,1,0:T(8,128)(2,1)S(1)} async-done(((bf16[128,8,512]{2,1,0:T(8,128)(2,1)}), bf16[128,8,512]{2,1,0:T(8,128)(2,1)S(1)}, u32[]{:S(2)}, u32[]{:S(2)}) %all-to-all-start.2) | async-done | bytes 1048608 | tf_op jit(solution)/shard_map/all_to_all | solution.py:378
  197.0 9.0 %scatter_custom_fusion.2 = f32[2048,512]{1,0:T(8,128)} fusion(s32[1024]{0:T(1024)S(1)} %reshape.130, f32[]{:T(128)} %constant.50.clone.1, bf16[128,8,512]{2,1,0:T(8,128)(2,1)S(1)} %all-to-all-done.2), kind=kCustom, calls=%fused_computation.5 | custom fusion | flops 1048576 | bytes 5242884 | tf_op jit(solution)/shard_map/scatter-add | solution.py:382
  206.0 124.4 %all-reduce.3.cloned.1.call-done = (f32[512,2048]{1,0:T(8,128)}, f32[512,512]{1,0:T(8,128)}) async-done(((f32[512,2048]{1,0:T(8,128)}, f32[512,512]{1,0:T(8,128)}), (f32[512,2048]{1,0:T(8,128)}, f32[512,512]{1,0:T(8,128)})) %all-reduce.3.cloned.1.call-update) | async-done | bytes 5242896 | tf_op jit(solution)/shard_map/psum | solution.py:384
  330.4 1.9 copy.33
  332.3 4.8 %copy.34 = f32[512,2048]{1,0:T(8,128)} copy(f32[512,2048]{1,0:T(8,128)} %get-tuple-element.22) | data formatting | bytes 8388608
  337.0 1.0 copy.35
  (14 shorter events, 0.2 us)
Async XLA Ops:
  7.2 27.0 %copy-start = (bf16[2048,512]{1,0:T(8,128)(2,1)S(1)}, bf16[2048,512]{1,0:T(8,128)(2,1)}, u32[]{:S(2)}) copy-start(bf16[2048,512]{1,0:T(8,128)(2,1)} %param.9) | copy-start | bytes 6291460
  38.2 6.5 %copy-start.2 = (s32[1,512,1]{1,2,0:T(1,128)S(1)}, s32[1,512,1]{1,2,0:T(1,128)}, u32[]{:S(2)}) copy-start(s32[1,512,1]{1,2,0:T(1,128)} %param.10) | copy-start | bytes 6148
  39.4 23.7 %all-to-all-start.1 = ((bf16[128,8,512]{2,1,0:T(8,128)(2,1)}), bf16[128,8,512]{2,1,0:T(8,128)(2,1)S(1)}, u32[]{:S(2)}, u32[]{:S(2)}) async-start(bf16[128,8,512]{2,1,0:T(8,128)(2,1)} %fusion.4), calls=%async_computation.1 | async-start | bytes 2097152 | tf_op jit(solution)/shard_map/all_to_all | solution.py:372
  43.9 286.5 %all-reduce.3.cloned.1.call-start = ((), (), s32[]{:S(2)}) async-start(), calls=%async_computation.3 | async-start | bytes 10485760 | tf_op jit(solution)/shard_map/psum | solution.py:384
  159.8 37.2 %all-to-all-start.2 = ((bf16[128,8,512]{2,1,0:T(8,128)(2,1)}), bf16[128,8,512]{2,1,0:T(8,128)(2,1)S(1)}, u32[]{:S(2)}, u32[]{:S(2)}) async-start(bf16[128,8,512]{2,1,0:T(8,128)(2,1)} %bitcast.18), calls=%async_computation.2 | async-start | bytes 2097152 | tf_op jit(solution)/shard_map/all_to_all | solution.py:378
  332.3 4.8 %copy-start.1 = (f32[512,512]{1,0:T(8,128)S(1)}, f32[512,512]{1,0:T(8,128)}, u32[]{:S(2)}) copy-start(f32[512,512]{1,0:T(8,128)} %get-tuple-element.23) | copy-start | bytes 3145732
Sparse Core Ops, SparseCore 0:
  156.0 174.3 all-reduce.2

commit v2 on v1

--- a/solution.py
+++ b/solution.py
@@ -30,7 +30,7 @@
 def layer_kernel(
     factor,
     len_ref, x_ref, og_ref, gin_ref, gout_ref, w_in_ref, w_out_ref,
-    hidden_ref, egrad_ref, interm_ref, outterm_ref,
+    hidden_ref, egrad_ref, terms_ref,
     normed, normed_t, slope, gate, upstream, joined, jgrad, nback, pback,
     q_out, kv_out, q_in, kv_in, mix_out, mix_in, dm_out, dm_in,
     dq_acc, dkv_acc, part_out, part_in, dq_out, dkv_out, dq_in, dkv_in, m_acc,
@@ -167,7 +167,15 @@
             return c
 
         lax.fori_loop(0, i, inner, 0)
-        mix_out[k] = m_acc[...].astype(BF)
+        m = m_acc[...]
+        shift = jnp.mean(m, -1, keepdims=True).astype(BF).astype(F32)
+        mix_out[k, :TOK, :] = (m - shift).astype(BF)
+        wide = jnp.broadcast_to(shift, (TOK, HEAD))
+        lines = jnp.zeros((16, HEAD), F32)
+        line = lax.broadcasted_iota(jnp.int32, (16, HEAD), 0)
+        for b in range(TOK // HEAD):
+            lines += jnp.where(line == b, wide[b * HEAD : (b + 1) * HEAD].T[:16], 0.0)
+        mix_out[k, TOK:, :] = lines.astype(BF)
         push(mix_out.at[k], mix_in.at[head], mix_send.at[k], mix_recv.at[head], i, base + user_core)
         return carry
 
@@ -180,7 +188,10 @@
         start = pl.multiple_of(r * TILE, TILE)
         rows = pl.ds(start, TILE)
         alive = live_rows(start, TILE)
-        m = jnp.concatenate([mix_in[h, rows, :] for h in range(HEADS)], axis=1).astype(F32) * alive
+        pick = (lax.broadcasted_iota(jnp.int32, (16, HEAD), 0) == r).astype(F32).astype(BF)
+        m = jnp.concatenate(
+            [mix_in[h, rows, :].astype(F32) + dot(mix_in[h, TOK:, :], pick, 0, 0) for h in range(HEADS)], axis=1
+        ) * alive
         mean = jnp.mean(m, -1, keepdims=True)
         cent = m - mean
         var = jnp.mean(cent * cent, -1, keepdims=True)
@@ -203,8 +214,8 @@
         push(dm_out.at[h], dm_in.at[slot_of_s], dm_send.at[h], dm_recv.at[slot_of_s], *worker(h))
 
     hidden_ref[...] = ((dot(joined[...], w_out_ref[...]) + x_ref[...].astype(F32)) * live).astype(BF)
-    outterm_ref[...] = dot(joined[...], upstream[...], 0, 0) * factor
-    interm_ref[:, :WIDTH] = dot(normed_t[...], pback[:, :WIDTH]) * factor
+    terms_ref[4] = (dot(joined[...], upstream[...], 0, 0) * factor).astype(BF)
+    terms_ref[0] = (dot(normed_t[...], pback[:, :WIDTH]) * factor).astype(BF)
     nback[...] = dot(pback[:, :WIDTH], w_in_ref[:, :WIDTH], 1, 1)
 
     for k in range(4):
@@ -299,11 +310,11 @@
     lax.fori_loop(0, TOK // TILE, back_tile, 0)
 
     def in_columns(c, carry):
-        cols = pl.ds(pl.multiple_of(c * 256, 256), 256)
-        interm_ref[:, cols] = dot(normed_t[...], pback[:, cols]) * factor
-        return carry
-
-    lax.fori_loop(2, 8, in_columns, 0)
+        cols = pl.ds(pl.multiple_of(c * WIDTH, WIDTH), WIDTH)
+        terms_ref[c] = (dot(normed_t[...], pback[:, cols]) * factor).astype(BF)
+        return carry
+
+    lax.fori_loop(1, 4, in_columns, 0)
 
     for h in range(HEADS):
         to = worker(h)
@@ -329,7 +340,7 @@
         buf(TOK, WIDTH), buf(WIDTH, TOK), buf(TOK, 4 * WIDTH, dtype=F32), buf(TOK, WIDTH), buf(TOK, WIDTH),
         buf(TOK, WIDTH), buf(TOK, WIDTH, dtype=F32), buf(TOK, WIDTH, dtype=F32), buf(TOK, 4 * WIDTH),
         buf(4, TOK, HEAD), buf(4, TOK, 2 * HEAD), buf(4, TOK, HEAD), buf(8, TOK, 2 * HEAD),
-        buf(4, TOK, HEAD), buf(4, TOK, HEAD), buf(4, TOK, HEAD), buf(4, TOK, HEAD),
+        buf(4, TOK + 16, HEAD), buf(4, TOK + 16, HEAD), buf(4, TOK, HEAD), buf(4, TOK, HEAD),
         buf(4, TOK, HEAD, dtype=F32), buf(8, TOK, 2 * HEAD, dtype=F32),
         buf(4, TOK, 2 * HEAD), buf(4, TOK, 2 * HEAD), buf(4, TOK, HEAD), buf(4, TOK, 2 * HEAD),
         buf(4, TOK, HEAD), buf(4, TOK, 2 * HEAD), buf(TOK, HEAD, dtype=F32),
@@ -340,11 +351,10 @@
         out_shape=(
             jax.ShapeDtypeStruct((TOK, WIDTH), BF),
             jax.ShapeDtypeStruct((TOK, WIDTH), BF),
-            jax.ShapeDtypeStruct((WIDTH, 4 * WIDTH), F32),
-            jax.ShapeDtypeStruct((WIDTH, WIDTH), F32),
+            jax.ShapeDtypeStruct((5, WIDTH, WIDTH), BF),
         ),
         in_specs=[pl.BlockSpec(memory_space=pltpu.SMEM)] + [vm] * 6,
-        out_specs=(vm,) * 4,
+        out_specs=(vm,) * 3,
         scratch_shapes=blocks + sems,
         compiler_params=pltpu.CompilerParams(
             collective_id=0, has_side_effects=True, vmem_limit_bytes=56 * 1024 * 1024
@@ -353,36 +363,373 @@
     )(length, embed, out_grad, gain_in.reshape(1, -1), gain_out.reshape(1, -1), w_in, w_out)
 
 
+OWNERS = 128
+SLOTS = 8
+ROWS = 2048
+
+
+def greet_all(s, t):
+    barrier = pltpu.get_barrier_semaphore()
+    me = s * 16 + t
+
+    def greet(d, carry):
+        other = lax.rem(me + d, OWNERS)
+        pl.semaphore_signal(
+            barrier, inc=1, device_id=(other // 16, lax.rem(other, 16)), device_id_type=MESH
+        )
+        return carry
+
+    lax.fori_loop(1, OWNERS, greet, 0)
+    pl.semaphore_wait(barrier, OWNERS - 1)
+
+
+def send_rows(src, dst, send, recv, s, t, to_s, to_t, take, place):
+    mine = jnp.logical_and(to_s == s, to_t == t)
+
+    @pl.when(mine)
+    def _():
+        pltpu.make_async_copy(src.at[take], dst.at[place], recv).start()
+
+    @pl.when(jnp.logical_not(mine))
+    def _():
+        pltpu.make_async_remote_copy(
+            src_ref=src.at[take], dst_ref=dst.at[place], send_sem=send, recv_sem=recv,
+            device_id=(to_s, to_t), device_id_type=MESH,
+        ).start()
+
+
+def sixteen(index):
+    return pl.ds(pl.multiple_of(index * 16, 16), 16)
+
+
+def spread(src, dst, send, recv, s, t, to_s):
+    def one(p, carry):
+        to_t = lax.rem(t + p, 16)
+        send_rows(src, dst, send, recv, s, t, to_s, to_t, sixteen(to_s * 16 + to_t), sixteen(s * 16 + t))
+        return carry
+
+    lax.fori_loop(0, 16, one, 0)
+
+
+def front_kernel(
+    owner_ref, row_ref, table_ref, embed_ref, slot_ref, asked_ref,
+    req_out, req_in, asked_col, found, fetched, req_send, req_recv, row_send, row_recv,
+):
+    s = lax.axis_index("seq")
+    t = lax.axis_index("table")
+    me = s * 16 + t
+    greet_all(s, t)
+
+    target = owner_ref[...]
+    lane = lax.broadcasted_iota(jnp.int32, (TOK, OWNERS), 1)
+    chosen_mask = lane == target
+    chosen = jnp.where(chosen_mask, 1.0, 0.0).astype(BF)
+    below = jnp.where(
+        lax.broadcasted_iota(jnp.int32, (TOK, TOK), 1) < lax.broadcasted_iota(jnp.int32, (TOK, TOK), 0), 1.0, 0.0
+    ).astype(BF)
+    before = dot(below, chosen)
+    rank = jnp.sum(jnp.where(chosen_mask, before, 0.0), axis=1, keepdims=True).astype(jnp.int32)
+    value = row_ref[...] + 1
+    high = (value >> 7).astype(F32)
+    low = (value & 127).astype(F32)
+    message = jnp.where(lane == rank, high, 0.0) + jnp.where(lane == rank + SLOTS, low, 0.0)
+    req_out[:, 0, :] = dot(chosen, message.astype(BF), 0, 0)
+
+    def ask(p, carry):
+        other = lax.rem(me + p, OWNERS)
+        send_rows(
+            req_out, req_in, req_send, req_recv, s, t, other // 16, lax.rem(other, 16), other, me
+        )
+        return carry
+
+    lax.fori_loop(0, OWNERS, ask, 0)
+
+    place = target * 16 + rank
+    slot_ref[...] = jnp.broadcast_to(place.astype(F32), (TOK, 128)).T[:8]
+
+    landed(req_in, req_recv)
+    number = lax.broadcasted_iota(jnp.int32, (OWNERS * SLOTS, OWNERS), 0)
+    lane_s = lax.broadcasted_iota(jnp.int32, (OWNERS * SLOTS, OWNERS), 1)
+    expand = jnp.where((number >> 3) == lane_s, 1.0, 0.0).astype(BF)
+    values = dot(expand, req_in[:, 0, :].astype(BF))
+    own = number & 7
+    asked = (
+        jnp.sum(
+            jnp.where(lane_s == own, values * 128.0, 0.0) + jnp.where(lane_s == own + SLOTS, values, 0.0),
+            axis=1,
+            keepdims=True,
+        )
+        - 1.0
+    )
+    wide = jnp.broadcast_to(asked, (OWNERS * SLOTS, 128))
+    asked_col[...] = wide
+    asked_ref[...] = wide.T[:8]
+
+    def gather(p, carry):
+        q = lax.rem(s + p, 8)
+        column = asked_col[pl.ds(pl.multiple_of(q * 128, 128), 128), :][:, :1].astype(jnp.int32)
+        hit = lax.broadcasted_iota(jnp.int32, (128, ROWS), 1) == column
+        rows = dot(jnp.where(hit, 1.0, 0.0).astype(BF), table_ref[...])
+        both = jnp.concatenate(
+            [rows[:, :256].reshape(16, SLOTS, 256), rows[:, 256:].reshape(16, SLOTS, 256)], axis=1
+        )
+        found[pl.ds(pl.multiple_of(q * 256, 256), 256), :] = both.reshape(256, 256).astype(BF)
+        spread(found, fetched, row_send, row_recv, s, t, q)
+        return carry
+
+    lax.fori_loop(0, 8, gather, 0)
+    landed(fetched, row_recv)
+    for r in range(TOK // TILE):
+        rows = slice(r * TILE, (r + 1) * TILE)
+        at = lax.broadcasted_iota(jnp.int32, (TILE, ROWS), 1)
+        first = jnp.where(at == place[rows], 1.0, 0.0).astype(BF)
+        second = jnp.where(at == place[rows] + SLOTS, 1.0, 0.0).astype(BF)
+        embed_ref[rows, :256] = dot(first, fetched[...]).astype(BF)
+        embed_ref[rows, 256:] = dot(second, fetched[...]).astype(BF)
+    landed(req_out.at[pl.ds(0, OWNERS - 1)], req_send)
+    landed(found.at[pl.ds(0, (OWNERS - 1) * 16)], row_send)
+
+
+def front(owner, item_row, item_table):
+    vm = pl.BlockSpec(memory_space=pltpu.VMEM)
+    dma = pltpu.SemaphoreType.DMA
+    return pl.pallas_call(
+        front_kernel,
+        out_shape=(
+            jax.ShapeDtypeStruct((TOK, WIDTH), BF),
+            jax.ShapeDtypeStruct((8, TOK), F32),
+            jax.ShapeDtypeStruct((8, OWNERS * SLOTS), F32),
+        ),
+        in_specs=[vm] * 3,
+        out_specs=(vm,) * 3,
+        scratch_shapes=[
+            pltpu.VMEM((OWNERS, 1, 128), F32), pltpu.VMEM((OWNERS, 1, 128), F32),
+            pltpu.VMEM((OWNERS * SLOTS, 128), F32),
+            pltpu.VMEM((ROWS, 256), BF), pltpu.VMEM((ROWS, 256), BF),
+            dma, dma, dma, dma,
+        ],
+        compiler_params=pltpu.CompilerParams(
+            collective_id=1, has_side_effects=True, vmem_limit_bytes=48 * 1024 * 1024
+        ),
+    )(owner, item_row, item_table)
+
+
+ORDERS = ("xyz", "yzx", "zxy", "xzy", "yxz")
+
+
+def tail_kernel(
+    egrad_ref, slot_ref, terms_ref, incoming_ref, sums_ref,
+    outgoing, r0, a1, r1, a2, r2, a3, r3,
+    row_send, row_recv, s0, v0, s1, v1, s2, v2, s3, v3, s4, v4, s5, v5, s6, v6, s7, v7,
+):
+    s = lax.axis_index("seq")
+    t = lax.axis_index("table")
+    core = lax.rem(t, 2)
+    x, z = lax.rem(s, 4), t // 4
+    y = lax.rem(t // 2, 2) * 2 + s // 4
+    sibling = t + 1 - 2 * core
+    greet_all(s, t)
+
+    place = {"x": x, "y": y, "z": z}
+
+    def partner(axis, d):
+        other = lax.rem(place[axis] + d, 4)
+        if axis == "x":
+            return other, s - x + other, t
+        if axis == "y":
+            return other, lax.rem(other, 2) * 4 + x, z * 4 + (other // 2) * 2 + core
+        return other, s, other * 4 + lax.rem(t, 4)
+
+    def ship(src, dst, send, recv, to_s, to_t):
+        pltpu.make_async_remote_copy(
+            src_ref=src, dst_ref=dst, send_sem=send, recv_sem=recv,
+            device_id=(to_s, to_t), device_id_type=MESH,
+        ).start()
+
+    units = range(len(ORDERS))
+    half = pl.ds(pl.multiple_of(core * 256, 256), 256)
+    other_half = pl.ds(pl.multiple_of(256 - core * 256, 256), 256)
+    for u in units:
+        ship(terms_ref.at[u, other_half], r0.at[u], s0.at[u], v0.at[u], s, sibling)
+
+    slot = slot_ref[...][:1].astype(jnp.int32)
+
+    def scatter(p, carry):
+        q = lax.rem(s + p, 8)
+        at = lax.broadcasted_iota(jnp.int32, (256, TOK), 0) + q * 256
+        first = jnp.where(at == slot, 1.0, 0.0).astype(BF)
+        second = jnp.where(at == slot + SLOTS, 1.0, 0.0).astype(BF)
+        outgoing[pl.ds(pl.multiple_of(q * 256, 256), 256), :] = (
+            dot(first, egrad_ref[:, :256]) + dot(second, egrad_ref[:, 256:])
+        ).astype(BF)
+        spread(outgoing, incoming_ref, row_send, row_recv, s, t, q)
+        return carry
+
+    lax.fori_loop(0, 8, scatter, 0)
+
+    def block(axis, size):
+        return pl.ds(pl.multiple_of(place[axis] * size, size), size)
+
+    def block_of(index, size):
+        return pl.ds(pl.multiple_of(index * size, size), size)
+
+    for u in units:
+        landed(r0.at[u], v0.at[u])
+        a1[u] = (terms_ref[u, half, :].astype(F32) + r0[u].astype(F32)).astype(BF)
+        for d in range(1, 4):
+            other, to_s, to_t = partner(ORDERS[u][0], d)
+            ship(a1.at[u, block_of(other, 64)], r1.at[u, d - 1], s1.at[u, d - 1], v1.at[u, d - 1], to_s, to_t)
+    for u in units:
+        total = a1[u, block(ORDERS[u][0], 64), :].astype(F32)
+        for d in range(1, 4):
+            landed(r1.at[u, d - 1], v1.at[u, d - 1])
+            total += r1[u, d - 1].astype(F32)
+        a2[u] = total.astype(BF)
+        for d in range(1, 4):
+            other, to_s, to_t = partner(ORDERS[u][1], d)
+            ship(a2.at[u, block_of(other, 16)], r2.at[u, d - 1], s2.at[u, d - 1], v2.at[u, d - 1], to_s, to_t)
+    for u in units:
+        total = a2[u, block(ORDERS[u][1], 16), :].astype(F32)
+        for d in range(1, 4):
+            landed(r2.at[u, d - 1], v2.at[u, d - 1])
+            total += r2[u, d - 1].astype(F32)
+        a3[u] = total.astype(BF)
+        for d in range(1, 4):
+            other, to_s, to_t = partner(ORDERS[u][2], d)
+            ship(
+                a3.at[u, :, block_of(other, 128)], r3.at[u, d - 1], s3.at[u, d - 1], v3.at[u, d - 1], to_s, to_t
+            )
+
+    def spot(u, first, second, third):
+        return sums_ref.at[u, pl.ds(pl.multiple_of(core * 256 + first * 64 + second * 16, 16), 16), block_of(third, 128)]
+
+    def lines(u, first, second):
+        return sums_ref.at[u, pl.ds(pl.multiple_of(core * 256 + first * 64 + second * 16, 16), 16)]
+
+    def quarter(u, first):
+        return sums_ref.at[u, pl.ds(pl.multiple_of(core * 256 + first * 64, 64), 64)]
+
+    def before(axis, d):
+        return lax.rem(place[axis] + 4 - d, 4)
+
+    for u in units:
+        one, two, three = ORDERS[u]
+        total = a3[u, :, block(three, 128)].astype(F32)
+        for d in range(1, 4):
+            landed(r3.at[u, d - 1], v3.at[u, d - 1])
+            total += r3[u, d - 1].astype(F32)
+        mine = spot(u, place[one], place[two], place[three])
+        mine[...] = total.astype(BF)
+        for d in range(1, 4):
+            _, to_s, to_t = partner(three, d)
+            ship(mine, mine, s4.at[u, d - 1], v4.at[u, d - 1], to_s, to_t)
+    for u in units:
+        one, two, three = ORDERS[u]
+        for d in range(1, 4):
+            landed(spot(u, place[one], place[two], before(three, d)), v4.at[u, d - 1])
+        mine = lines(u, place[one], place[two])
+        for d in range(1, 4):
+            _, to_s, to_t = partner(two, d)
+            ship(mine, mine, s5.at[u, d - 1], v5.at[u, d - 1], to_s, to_t)
+    for u in units:
+        one, two, three = ORDERS[u]
+        for d in range(1, 4):
+            landed(lines(u, place[one], before(two, d)), v5.at[u, d - 1])
+        mine = quarter(u, place[one])
+        for d in range(1, 4):
+            _, to_s, to_t = partner(one, d)
+            ship(mine, mine, s6.at[u, d - 1], v6.at[u, d - 1], to_s, to_t)
+    for u in units:
+        one, two, three = ORDERS[u]
+        for d in range(1, 4):
+            landed(quarter(u, before(one, d)), v6.at[u, d - 1])
+        ship(sums_ref.at[u, half], sums_ref.at[u, half], s7.at[u], v7.at[u], s, sibling)
+    for u in units:
+        landed(sums_ref.at[u, other_half], v7.at[u])
+
+    landed(incoming_ref, row_recv)
+    landed(outgoing.at[pl.ds(0, (OWNERS - 1) * 16)], row_send)
+    for u in units:
+        one, two, three = ORDERS[u]
+        landed(terms_ref.at[u, other_half], s0.at[u])
+        landed(sums_ref.at[u, half], s7.at[u])
+        for d in range(3):
+            landed(r1.at[u, d], s1.at[u, d])
+            landed(r2.at[u, d], s2.at[u, d])
+            landed(r3.at[u, d], s3.at[u, d])
+            landed(spot(u, place[one], place[two], place[three]), s4.at[u, d])
+            landed(lines(u, place[one], place[two]), s5.at[u, d])
+            landed(quarter(u, place[one]), s6.at[u, d])
+
+
+def tail(embed_grad, slots, terms):
+    vm = pl.BlockSpec(memory_space=pltpu.VMEM)
+    dma = pltpu.SemaphoreType.DMA
+    n = len(ORDERS)
+    one, three = dma((n,)), dma((n, 3))
+
+    def buf(*shape):
+        return pltpu.VMEM(shape, BF)
+
+    return pl.pallas_call(
+        tail_kernel,
+        out_shape=(
+            jax.ShapeDtypeStruct((ROWS, 256), BF),
+            jax.ShapeDtypeStruct((n, WIDTH, WIDTH), BF),
+        ),
+        in_specs=[vm] * 3,
+        out_specs=(vm,) * 2,
+        scratch_shapes=[
+            buf(ROWS, 256), buf(n, 256, WIDTH), buf(n, 256, WIDTH), buf(n, 3, 64, WIDTH), buf(n, 64, WIDTH),
+            buf(n, 3, 16, WIDTH), buf(n, 16, WIDTH), buf(n, 3, 16, 128),
+            dma, dma, one, one, three, three, three, three, three, three,
+            three, three, three, three, three, three, one, one,
+        ],
+        compiler_params=pltpu.CompilerParams(
+            collective_id=2, has_side_effects=True, vmem_limit_bytes=48 * 1024 * 1024
+        ),
+    )(embed_grad, slots, terms)
+
+
+def table_kernel(incoming_ref, asked_ref, out_ref, rows):
+    @pl.when(pl.program_id(0) == 0)
+    def _():
+        for q in range(8):
+            both = incoming_ref[q * 256 : (q + 1) * 256, :].astype(F32).reshape(16, 16, 256)
+            part = slice(q * 128, (q + 1) * 128)
+            rows[part, :256] = both[:, :SLOTS].reshape(128, 256).astype(BF)
+            rows[part, 256:] = both[:, SLOTS:].reshape(128, 256).astype(BF)
+
+    at = lax.broadcasted_iota(jnp.int32, (256, OWNERS * SLOTS), 0) + pl.program_id(0) * 256
+    hit = at == asked_ref[...][:1].astype(jnp.int32)
+    out_ref[...] = dot(jnp.where(hit, 1.0, 0.0).astype(BF), rows[...])
+
+
+def table_sum(incoming, asked):
+    return pl.pallas_call(
+        table_kernel,
+        grid=(8,),
+        out_shape=jax.ShapeDtypeStruct((ROWS, WIDTH), F32),
+        in_specs=[
+            pl.BlockSpec((ROWS, 256), lambda i: (0, 0)),
+            pl.BlockSpec((8, OWNERS * SLOTS), lambda i: (0, 0)),
+        ],
+        out_specs=pl.BlockSpec((256, WIDTH), lambda i: (i, 0)),
+        scratch_shapes=[pltpu.VMEM((OWNERS * SLOTS, WIDTH), BF)],
+        compiler_params=pltpu.CompilerParams(vmem_limit_bytes=32 * 1024 * 1024),
+    )(incoming, asked)
+
+
 def local(item_table, owner, item_row, lengths, gain_in, gain_out, w_in, w_out, out_grad):
-    events_here = owner.shape[1]
-    owners = lax.axis_size(("seq", "table"))
-    slots = max(2, 2 * events_here // owners)
-    width = w_out.shape[0]
-    factor = (events_here * owners) ** (-0.5)
-    target = owner[0, :, 0]
-    wanted = item_row[0]
-    chosen = (target[:, None] == jnp.arange(owners, dtype=jnp.int32)[None, :]).astype(jnp.int32)
-    before = jnp.cumsum(chosen, axis=0) - chosen
-    rank = jnp.sum(before * chosen, axis=1)
-    slot = target * slots + rank
-    request = jnp.full((owners * slots,), -1, jnp.int32).at[slot].set(wanted).reshape(owners, slots)
-    asked = lax.all_to_all(request, ("seq", "table"), split_axis=0, concat_axis=0, tiled=True)
-    found = jnp.take(item_table, jnp.maximum(asked, 0), axis=0)
-    found = jnp.where((asked >= 0)[:, :, None], found, jnp.zeros_like(found))
-    fetched = lax.all_to_all(found, ("seq", "table"), split_axis=0, concat_axis=0, tiled=True)
-    embed = jnp.take(fetched.reshape(owners * slots, width), slot, axis=0)
-    hidden, embed_grad, in_term, out_term = layer(
+    factor = (TOK * OWNERS) ** (-0.5)
+    embed, slots, asked = front(owner[0], item_row.reshape(TOK, 1), item_table)
+    hidden, embed_grad, terms = layer(
         lengths, embed, out_grad[0], gain_in, gain_out, w_in, w_out, factor
     )
-    outgoing = jnp.zeros((owners * slots, width), jnp.bfloat16).at[slot].set(embed_grad).reshape(owners, slots, width)
-    incoming = lax.all_to_all(outgoing, ("seq", "table"), split_axis=0, concat_axis=0, tiled=True)
-    table_grad = (
-        jnp.zeros((item_table.shape[0], width), jnp.float32)
-        .at[jnp.maximum(asked, 0).reshape(-1)]
-        .add(incoming.reshape(-1, width).astype(jnp.float32))
-    )
-    w_in_grad, w_out_grad = lax.psum((in_term, out_term), ("seq", "table"))
-    return (hidden[None], table_grad, w_in_grad, w_out_grad)
+    incoming, sums = tail(embed_grad, slots, terms)
+    table_grad = table_sum(incoming, asked)
+    w_in_grad = jnp.concatenate([sums[u] for u in range(4)], axis=1).astype(F32)
+    return (hidden[None], table_grad, w_in_grad, sums[4].astype(F32))
 
 
 def solution(mesh):

time: 345 us -> 210 us (0.61)
  waiting for transfers between devices: 163 us -> 0 us
  Pallas kernels: 88.2 us -> 198 us
  starting transfers between devices: 22.1 us -> 0 us
  blocking collectives: 20.9 us -> 0 us
  local copies, waits for them, and re-layouts: 22.3 us -> 5.85 us
  between operations: 14.8 us -> 1.35 us
  other arithmetic: 14.1 us -> 3.83 us
    psum x1 -> x0, waiting for transfers between devices: 124 us -> none  [local(): w_in_grad, w_out_grad = lax.psum((in_term, out_term), ('seq', 'table'))]
    pallas_call x0 -> x3, Pallas kernels: none -> 109 us  [the longest x1 64.5 us: tail(): pl.pallas_call(tail_kernel, out_shape=(jax.ShapeDtypeStruct((ROWS, 256),...]
    all_to_all x2 -> x0, waiting for transfers between devices: 38.1 us -> none  [the longest x1 19.7 us: local(): lax.all_to_all(outgoing, ('seq', 'table'), split_axis=0, concat_axis=0, t...]
    all_to_all x2 -> x0, starting transfers between devices: 22 us -> none  [the longest x1 17.5 us: local(): lax.all_to_all(outgoing, ('seq', 'table'), split_axis=0, concat_axis=0, t...]
    all_to_all x1 -> x0, blocking collectives: 20.9 us -> none  [local(): lax.all_to_all(request, ('seq', 'table'), split_axis=0, concat_axis=0, ti...]
    scatter-add x1 -> x0, other arithmetic: 8.95 us -> none  [local(): table_grad = jnp.zeros((item_table.shape[0], width), jnp.float32).at[jnp....]
    gather x2 -> x0, local copies, waits for them, and re-layouts: 6.58 us -> none  [the longest x1 3.97 us: local(): found = jnp.take(item_table, jnp.maximum(asked, 0), axis=0)]
    scatter x2 -> x0, local copies, waits for them, and re-layouts: 6.55 us -> none  [the longest x1 3.95 us: local(): jnp.zeros((owners * slots, width), jnp.bfloat16).at[slot].set(embed_grad)]
  transfers between devices with their start and end apart: 3 -> 0, of which waited for: 3 -> 0; matrix products, arithmetic and copies ran while one was open for 4% -> 0% of each run, Pallas kernels for 0% -> 0%
where the time goes in v2:
time: 210 us; the launch traced here: 209 us
  Pallas kernels  198 us (94%)
  local copies, waits for them, and re-layouts  5.85 us (3%)
  other arithmetic  3.83 us (2%)
    pallas_call x1, Pallas kernels, layer(): pl.pallas_call(functools.partial(layer_kernel, factor), out_shape=(jax.Sh...  89.7 us
    pallas_call x1, Pallas kernels, tail(): pl.pallas_call(tail_kernel, out_shape=(jax.ShapeDtypeStruct((ROWS, 256),...  64.5 us
    pallas_call x1, Pallas kernels, front(): pl.pallas_call(front_kernel, out_shape=(jax.ShapeDtypeStruct((TOK, WIDTH)...  38.8 us
    pallas_call x1, Pallas kernels, table_sum(): pl.pallas_call(table_kernel, grid=(8,), out_shape=jax.ShapeDtypeStruct((R...  5.44 us
    unnamed x9, local copies, waits for them, and re-layouts  4.21 us

profile of v2, /device:TPU:1, one launch (start us, length us, event | category | flops | bytes accessed | tf_op | source)
XLA Modules:
  0.0 209.5 jit_solution(8678219231220958773)
XLA Ops:
  0.6 0.8 copy.13.owner_ref
  1.5 0.8 copy.14.row_ref
  2.3 0.0 copy-start
  2.3 1.6 copy-done
  3.9 38.8 %shard_map.120 = (bf16[512,512]{1,0:T(8,128)(2,1)S(1)}, f32[8,512]{1,0:T(8,128)S(1)}, f32[8,1024]{1,0:T(8,128)S(1)}) custom-call(s32[512,1]{1,0:T(8,128)S(1)} %copy.13.owner_ref, s32[512,1]{1,0:T(8,128)S(1)} %copy.14.row_ref, bf16[2048,512]{1,0:T(8,128)(2,1)S(1)} %copy-done), custom_call_target="tpu_custom_call" | custom-call | tf_op jit(solution)/shard_map/pallas_call | solution.py:496
  42.6 0.0 copy-start.2
  42.7 0.8 copy-done.2
  44.1 89.7 %shard_map.121 = (bf16[512,512]{1,0:T(8,128)(2,1)}, bf16[512,512]{1,0:T(8,128)(2,1)}, bf16[5,512,512]{2,1,0:T(8,128)(2,1)}) custom-call(s32[1]{0:T(128)S(6)} %copy.16.len_ref, bf16[512,512]{1,0:T(8,128)(2,1)} %copy-done.2, bf16[512,512]{1,0:T(8,128)(2,1)} %bitcast.20, f32[1,512]{1,0:T(1,128)} %bitcast.21, f32[1,512]{1,0:T(1,128)} %bitcast.22, ...), custom_call_target="tpu_custom_call" | custom-call | flops 14000000000 | bytes 12582912 | tf_op jit(solution)/shard_map/pallas_call | solution.py:349
  133.8 0.0 copy-start.1
  133.8 1.0 copy-done.1
  134.9 64.5 %shard_map.122 = (bf16[2048,256]{1,0:T(8,128)(2,1)S(1)}, bf16[5,512,512]{2,1,0:T(8,128)(2,1)S(1)}) custom-call(bf16[512,512]{1,0:T(8,128)(2,1)S(1)} %copy-done.1, f32[8,512]{1,0:T(8,128)S(1)} %get-tuple-element.15.slot_ref, bf16[5,512,512]{2,1,0:T(8,128)(2,1)} %get-tuple-element.16.terms_ref), custom_call_target="tpu_custom_call" | custom-call | tf_op jit(solution)/shard_map/pallas_call | solution.py:674
  199.4 1.3 bitcast_convert_fusion
  200.7 2.6 %maximum_convert_fusion = f32[512,2048]{1,0:T(8,128)} fusion(bf16[512,512]{1,0:T(8,128)(2,1)S(1)} %get-tuple-element.21, bf16[512,512]{1,0:T(8,128)(2,1)S(1)} %get-tuple-element.22, bf16[512,512]{1,0:T(8,128)(2,1)S(1)} %get-tuple-element.23, bf16[512,512]{1,0:T(8,128)(2,1)S(1)} %get-tuple-element.24), kind=kLoop, calls=%fused_computation | loop fusion | flops 8388608 | bytes 6291456 | tf_op jit(solution)/shard_map/convert_element_type | solution.py:731
  203.2 0.0 copy-start.3
  203.2 5.4 %shard_map.123 = f32[2048,512]{1,0:T(8,128)} custom-call(bf16[2048,256]{1,0:T(8,128)(2,1)S(1)} %get-tuple-element.17.incoming_ref, f32[8,1024]{1,0:T(8,128)S(1)} %get-tuple-element.18.asked_ref), custom_call_target="tpu_custom_call" | custom-call | tf_op jit(solution)/shard_map/pallas_call | solution.py:709
  208.7 0.0 copy-done.3
  208.7 0.8 copy.17
Async XLA Ops:
  2.3 1.6 copy-start
  42.6 0.8 copy-start.2
  133.8 1.0 copy-start.1
  203.2 5.4 %copy-start.3 = (bf16[512,512]{1,0:T(8,128)(2,1)S(1)}, bf16[512,512]{1,0:T(8,128)(2,1)}, u32[]{:S(2)}) copy-start(bf16[512,512]{1,0:T(8,128)(2,1)} %get-tuple-element.13) | copy-start | bytes 1572868

commit v3 on v1

--- a/solution.py
+++ b/solution.py
@@ -27,18 +27,76 @@
     pltpu.make_async_copy(ref, ref, sem).wait()
 
 
-def layer_kernel(
+OWNERS = 128
+SLOTS = 8
+ROWS = 2048
+
+
+def greet_all(s, t):
+    barrier = pltpu.get_barrier_semaphore()
+    me = s * 16 + t
+
+    def greet(d, carry):
+        other = lax.rem(me + d, OWNERS)
+        pl.semaphore_signal(
+            barrier, inc=1, device_id=(other // 16, lax.rem(other, 16)), device_id_type=MESH
+        )
+        return carry
+
+    lax.fori_loop(1, OWNERS, greet, 0)
+    return barrier
+
+
+def send_rows(src, dst, send, recv, s, t, to_s, to_t, take, place):
+    mine = jnp.logical_and(to_s == s, to_t == t)
+
+    @pl.when(mine)
+    def _():
+        pltpu.make_async_copy(src.at[take], dst.at[place], recv).start()
+
+    @pl.when(jnp.logical_not(mine))
+    def _():
+        pltpu.make_async_remote_copy(
+            src_ref=src.at[take], dst_ref=dst.at[place], send_sem=send, recv_sem=recv,
+            device_id=(to_s, to_t), device_id_type=MESH,
+        ).start()
+
+
+def sixteen(index):
+    return pl.ds(pl.multiple_of(index * 16, 16), 16)
+
+
+def spread(src, dst, send, recv, s, t, to_s):
+    def one(p, carry):
+        to_t = lax.rem(t + p, 16)
+        send_rows(src, dst, send, recv, s, t, to_s, to_t, sixteen(to_s * 16 + to_t), sixteen(s * 16 + t))
+        return carry
+
+    lax.fori_loop(0, 16, one, 0)
+
+
+ORDERS = ("zxy", "xyz", "yzx", "zxy", "zyx")
+EARLY = (0, 4)
+LATE = (1, 2, 3)
+
+
+def step_kernel(
     factor,
-    len_ref, x_ref, og_ref, gin_ref, gout_ref, w_in_ref, w_out_ref,
-    hidden_ref, egrad_ref, interm_ref, outterm_ref,
-    normed, normed_t, slope, gate, upstream, joined, jgrad, nback, pback,
+    len_ref, owner_ref, row_ref, table_ref, og_ref, gin_ref, gout_ref, w_in_ref, w_out_ref,
+    hidden_ref, incoming_ref, sums_ref, asked_ref,
+    x_ref, egrad, terms, normed, normed_t, slope, gate, upstream, joined, jgrad, nback, pback,
     q_out, kv_out, q_in, kv_in, mix_out, mix_in, dm_out, dm_in,
     dq_acc, dkv_acc, part_out, part_in, dq_out, dkv_out, dq_in, dkv_in, m_acc,
+    req_out, req_in, asked_col, found, fetched, spot_col, pick_one, pick_two, put_one, put_two,
+    r0, a1, r1, a2, r2, a3, r3,
     q_send, q_recv, kv_send, kv_recv, fwd_send, mix_send, mix_recv, dm_send, dm_recv,
     part_send, part_recv, dq_send, dq_recv, dkv_send, dkv_recv,
+    req_send, req_recv, row_send, row_recv, back_send, back_recv,
+    s0, v0, s1, v1, s2, v2, s3, v3, s4, v4, s5, v5, s6, v6, s7, v7,
 ):
     s = lax.axis_index("seq")
     t = lax.axis_index("table")
+    me = s * 16 + t
     core = lax.rem(t, 2)
     base = t - core
     head = lax.rem(s, HEADS)
@@ -46,19 +104,9 @@
     sibling = base + 1 - core
     part_of_s = lax.rem((s + 1) // 2, 2)
     slot_of_s = s // 2
-
-    barrier = pltpu.get_barrier_semaphore()
-    me = s * 2 + core
-
-    def greet(d, carry):
-        other = lax.rem(me + d, 16)
-        pl.semaphore_signal(
-            barrier, inc=1, device_id=(other // 2, base + lax.rem(other, 2)), device_id_type=MESH
-        )
-        return carry
-
-    lax.fori_loop(1, 16, greet, 0)
-    pl.semaphore_wait(barrier, 15)
+    cx, cz = lax.rem(s, 4), t // 4
+    cy = lax.rem(t // 2, 2) * 2 + s // 4
+    barrier = greet_all(s, t)
 
     def push(src, dst, send, recv, to_s, to_t):
         mine = jnp.logical_and(to_s == s, to_t == t)
@@ -94,8 +142,184 @@
         pos = s * TOK + start + lax.broadcasted_iota(jnp.int32, (count, 1), 0)
         return (pos < length).astype(F32)
 
+    place = {"x": cx, "y": cy, "z": cz}
+
+    def partner(axis, d):
+        other = lax.rem(place[axis] + d, 4)
+        if axis == "x":
+            return other, s - cx + other, t
+        if axis == "y":
+            return other, lax.rem(other, 2) * 4 + cx, cz * 4 + (other // 2) * 2 + core
+        return other, s, other * 4 + lax.rem(t, 4)
+
+    def ship(src, dst, send, recv, to_s, to_t):
+        pltpu.make_async_remote_copy(
+            src_ref=src, dst_ref=dst, send_sem=send, recv_sem=recv,
+            device_id=(to_s, to_t), device_id_type=MESH,
+        ).start()
+
+    half = pl.ds(pl.multiple_of(core * 256, 256), 256)
+    other_half = pl.ds(pl.multiple_of(256 - core * 256, 256), 256)
+
+    def block_of(index, size):
+        return pl.ds(pl.multiple_of(index * size, size), size)
+
+    def block(axis, size):
+        return block_of(place[axis], size)
+
+    def spot(u, first, second, third):
+        return sums_ref.at[u, block_of(core * 16 + first * 4 + second, 16), block_of(third, 128)]
+
+    def lines(u, first, second):
+        return sums_ref.at[u, block_of(core * 16 + first * 4 + second, 16)]
+
+    def quarter(u, first):
+        return sums_ref.at[u, block_of(core * 4 + first, 64)]
+
+    def before_me(axis, d):
+        return lax.rem(place[axis] + 4 - d, 4)
+
+    def step(u, n):
+        one, two, three = ORDERS[u]
+        if n == 0:
+            ship(terms.at[u, other_half], r0.at[u], s0.at[u], v0.at[u], s, sibling)
+        elif n == 1:
+            landed(r0.at[u], v0.at[u])
+            a1[u] = (terms[u, half, :].astype(F32) + r0[u].astype(F32)).astype(BF)
+            for d in range(1, 4):
+                other, to_s, to_t = partner(one, d)
+                ship(a1.at[u, block_of(other, 64)], r1.at[u, d - 1], s1.at[u, d - 1], v1.at[u, d - 1], to_s, to_t)
+        elif n == 2:
+            total = a1[u, block(one, 64), :].astype(F32)
+            for d in range(1, 4):
+                landed(r1.at[u, d - 1], v1.at[u, d - 1])
+                total += r1[u, d - 1].astype(F32)
+            a2[u] = total.astype(BF)
+            for d in range(1, 4):
+                other, to_s, to_t = partner(two, d)
+                ship(a2.at[u, block_of(other, 16)], r2.at[u, d - 1], s2.at[u, d - 1], v2.at[u, d - 1], to_s, to_t)
+        elif n == 3:
+            total = a2[u, block(two, 16), :].astype(F32)
+            for d in range(1, 4):
+                landed(r2.at[u, d - 1], v2.at[u, d - 1])
+                total += r2[u, d - 1].astype(F32)
+            a3[u] = total.astype(BF)
+            for d in range(1, 4):
+                other, to_s, to_t = partner(three, d)
+                ship(
+                    a3.at[u, :, block_of(other, 128)], r3.at[u, d - 1], s3.at[u, d - 1], v3.at[u, d - 1], to_s, to_t
+                )
+        elif n == 4:
+            total = a3[u, :, block(three, 128)].astype(F32)
+            for d in range(1, 4):
+                landed(r3.at[u, d - 1], v3.at[u, d - 1])
+                total += r3[u, d - 1].astype(F32)
+            mine = spot(u, place[one], place[two], place[three])
+            mine[...] = total.astype(BF)
+            for d in range(1, 4):
+                _, to_s, to_t = partner(three, d)
+                ship(mine, mine, s4.at[u, d - 1], v4.at[u, d - 1], to_s, to_t)
+        elif n == 5:
+            for d in range(1, 4):
+                landed(spot(u, place[one], place[two], before_me(three, d)), v4.at[u, d - 1])
+            mine = lines(u, place[one], place[two])
+            for d in range(1, 4):
+                _, to_s, to_t = partner(two, d)
+                ship(mine, mine, s5.at[u, d - 1], v5.at[u, d - 1], to_s, to_t)
+        elif n == 6:
+            for d in range(1, 4):
+                landed(lines(u, place[one], before_me(two, d)), v5.at[u, d - 1])
+            mine = quarter(u, place[one])
+            for d in range(1, 4):
+                _, to_s, to_t = partner(one, d)
+                ship(mine, mine, s6.at[u, d - 1], v6.at[u, d - 1], to_s, to_t)
+        elif n == 7:
+            for d in range(1, 4):
+                landed(quarter(u, before_me(one, d)), v6.at[u, d - 1])
+            ship(sums_ref.at[u, half], sums_ref.at[u, half], s7.at[u], v7.at[u], s, sibling)
+        else:
+            landed(sums_ref.at[u, other_half], v7.at[u])
+
+    target = owner_ref[...]
+    lane = lax.broadcasted_iota(jnp.int32, (TOK, OWNERS), 1)
+    chosen_mask = lane == target
+    chosen = jnp.where(chosen_mask, 1.0, 0.0).astype(BF)
+    below = jnp.where(
+        lax.broadcasted_iota(jnp.int32, (TOK, TOK), 1) < lax.broadcasted_iota(jnp.int32, (TOK, TOK), 0), 1.0, 0.0
+    ).astype(BF)
+    before = dot(below, chosen)
+    rank = jnp.sum(jnp.where(chosen_mask, before, 0.0), axis=1, keepdims=True).astype(jnp.int32)
+    value = row_ref[...] + 1
+    high = (value >> 7).astype(F32)
+    low = (value & 127).astype(F32)
+    message = jnp.where(lane == rank, high, 0.0) + jnp.where(lane == rank + SLOTS, low, 0.0)
+    req_out[:, 0, :] = dot(chosen, message.astype(BF), 0, 0)
+
+    pl.semaphore_wait(barrier, OWNERS - 1)
+
+    def ask(p, carry):
+        other = lax.rem(me + p, OWNERS)
+        send_rows(
+            req_out, req_in, req_send, req_recv, s, t, other // 16, lax.rem(other, 16), other, me
+        )
+        return carry
+
+    lax.fori_loop(0, OWNERS, ask, 0)
+
+    spot_of = target * 16 + rank
+    slot_row = jnp.broadcast_to(spot_of.astype(F32), (TOK, 128)).T[:1].astype(jnp.int32)
+    live = live_rows(0, TOK)
+    upstream[...] = (og_ref[...].astype(F32) * live).astype(BF)
+    jgrad[...] = dot(upstream[...], w_out_ref[...], 1, 1)
+    number = lax.broadcasted_iota(jnp.int32, (OWNERS * SLOTS, OWNERS), 0)
+    lane_s = lax.broadcasted_iota(jnp.int32, (OWNERS * SLOTS, OWNERS), 1)
+    expand = jnp.where((number >> 3) == lane_s, 1.0, 0.0).astype(BF)
+    landed(req_in, req_recv)
+    values = dot(expand, req_in[:, 0, :].astype(BF))
+    own = number & 7
+    asked = (
+        jnp.sum(
+            jnp.where(lane_s == own, values * 128.0, 0.0) + jnp.where(lane_s == own + SLOTS, values, 0.0),
+            axis=1,
+            keepdims=True,
+        )
+        - 1.0
+    )
+    wide = jnp.broadcast_to(asked, (OWNERS * SLOTS, 128))
+    asked_col[...] = wide
+    asked_ref[...] = wide.T[:8]
+
+    def gather(p, carry):
+        q = lax.rem(s + p, 8)
+        column = asked_col[pl.ds(pl.multiple_of(q * 128, 128), 128), :][:, :1].astype(jnp.int32)
+        hit = lax.broadcasted_iota(jnp.int32, (128, ROWS), 1) == column
+        rows = dot(jnp.where(hit, 1.0, 0.0).astype(BF), table_ref[...])
+        both = jnp.concatenate(
+            [rows[:, :256].reshape(16, SLOTS, 256), rows[:, 256:].reshape(16, SLOTS, 256)], axis=1
+        )
+        found[pl.ds(pl.multiple_of(q * 256, 256), 256), :] = both.reshape(256, 256).astype(BF)
+        spread(found, fetched, row_send, row_recv, s, t, q)
+        return carry
+
+    lax.fori_loop(0, 8, gather, 0)
+    def pick_tile(r, carry):
+        rows = pl.ds(pl.multiple_of(r * TILE, TILE), TILE)
+        at = lax.broadcasted_iota(jnp.int32, (TILE, ROWS), 1)
+        spots = spot_col[rows, :][:, :1]
+        pick_one[rows, :] = jnp.where(at == spots, 1.0, 0.0).astype(BF)
+        pick_two[rows, :] = jnp.where(at == spots + SLOTS, 1.0, 0.0).astype(BF)
+        return carry
+
+    spot_col[...] = jnp.broadcast_to(spot_of, (TOK, 128))
+    lax.fori_loop(0, TOK // TILE, pick_tile, 0)
+    dq_acc[...] = jnp.zeros_like(dq_acc)
+    dkv_acc[...] = jnp.zeros_like(dkv_acc)
+    landed(fetched, row_recv)
+
     def norm_tile(r, carry):
         rows = pl.ds(pl.multiple_of(r * TILE, TILE), TILE)
+        x_ref[rows, :256] = dot(pick_one[rows, :], fetched[...]).astype(BF)
+        x_ref[rows, 256:] = dot(pick_two[rows, :], fetched[...]).astype(BF)
         x = x_ref[rows, :].astype(F32)
         mean = jnp.mean(x, -1, keepdims=True)
         cent = x - mean
@@ -104,8 +328,6 @@
         return carry
 
     lax.fori_loop(0, TOK // TILE, norm_tile, 0)
-
-    live = live_rows(0, TOK)
 
     def project(first, columns):
         pre = dot(normed[...], w_in_ref[:, pl.ds(first, columns)])
@@ -124,11 +346,16 @@
 
     gate[:, :256] = project(0, 256).astype(BF)
     gate[:, 256:] = project(256, 256).astype(BF)
-    upstream[...] = (og_ref[...].astype(F32) * live).astype(BF)
-    jgrad[...] = dot(upstream[...], w_out_ref[...], 1, 1)
     normed_t[...] = normed[...].T
-    dq_acc[...] = jnp.zeros_like(dq_acc)
-    dkv_acc[...] = jnp.zeros_like(dkv_acc)
+
+    def scatter_tile(q, carry):
+        rows = pl.ds(pl.multiple_of(q * 256, 256), 256)
+        at = lax.broadcasted_iota(jnp.int32, (256, TOK), 0) + q * 256
+        put_one[rows, :] = jnp.where(at == slot_row, 1.0, 0.0).astype(BF)
+        put_two[rows, :] = jnp.where(at == slot_row + SLOTS, 1.0, 0.0).astype(BF)
+        return carry
+
+    lax.fori_loop(0, 8, scatter_tile, 0)
 
     def take(k):
         d = mine_of(k)
@@ -167,7 +394,15 @@
             return c
 
         lax.fori_loop(0, i, inner, 0)
-        mix_out[k] = m_acc[...].astype(BF)
+        m = m_acc[...]
+        shift = jnp.mean(m, -1, keepdims=True).astype(BF).astype(F32)
+        mix_out[k, :TOK, :] = (m - shift).astype(BF)
+        wide = jnp.broadcast_to(shift, (TOK, HEAD))
+        lines = jnp.zeros((16, HEAD), F32)
+        line = lax.broadcasted_iota(jnp.int32, (16, HEAD), 0)
+        for b in range(TOK // HEAD):
+            lines += jnp.where(line == b, wide[b * HEAD : (b + 1) * HEAD].T[:16], 0.0)
+        mix_out[k, TOK:, :] = lines.astype(BF)
         push(mix_out.at[k], mix_in.at[head], mix_send.at[k], mix_recv.at[head], i, base + user_core)
         return carry
 
@@ -180,7 +415,10 @@
         start = pl.multiple_of(r * TILE, TILE)
         rows = pl.ds(start, TILE)
         alive = live_rows(start, TILE)
-        m = jnp.concatenate([mix_in[h, rows, :] for h in range(HEADS)], axis=1).astype(F32) * alive
+        pick = (lax.broadcasted_iota(jnp.int32, (16, HEAD), 0) == r).astype(F32).astype(BF)
+        m = jnp.concatenate(
+            [mix_in[h, rows, :].astype(F32) + dot(mix_in[h, TOK:, :], pick, 0, 0) for h in range(HEADS)], axis=1
+        ) * alive
         mean = jnp.mean(m, -1, keepdims=True)
         cent = m - mean
         var = jnp.mean(cent * cent, -1, keepdims=True)
@@ -202,9 +440,11 @@
     for h in range(HEADS):
         push(dm_out.at[h], dm_in.at[slot_of_s], dm_send.at[h], dm_recv.at[slot_of_s], *worker(h))
 
+    terms[4] = (dot(joined[...], upstream[...], 0, 0) * factor).astype(BF)
+    terms[0] = (dot(normed_t[...], pback[:, :WIDTH]) * factor).astype(BF)
+    for u in EARLY:
+        step(u, 0)
     hidden_ref[...] = ((dot(joined[...], w_out_ref[...]) + x_ref[...].astype(F32)) * live).astype(BF)
-    outterm_ref[...] = dot(joined[...], upstream[...], 0, 0) * factor
-    interm_ref[:, :WIDTH] = dot(normed_t[...], pback[:, :WIDTH]) * factor
     nback[...] = dot(pback[:, :WIDTH], w_in_ref[:, :WIDTH], 1, 1)
 
     for k in range(4):
@@ -248,6 +488,13 @@
                 return cc
 
             lax.fori_loop(jnp.where(i > j, m, m + 1), 4, inner, 0)
+            for n in range(8):
+
+                @pl.when(j == n)
+                def _():
+                    for u in EARLY:
+                        step(u, n + 1)
+
             return c
 
         lax.fori_loop(0, 2, one, 0)
@@ -272,7 +519,7 @@
         landed(dq_in.at[h], dq_recv.at[h])
         landed(dkv_in.at[h], dkv_recv.at[h])
 
-    def back_tile(r, carry):
+    def gate_tile(r, carry):
         start = pl.multiple_of(r * TILE, TILE)
         rows = pl.ds(start, TILE)
         alive = live_rows(start, TILE)
@@ -284,6 +531,15 @@
             ):
                 c = first + h * HEAD
                 pback[rows, c : c + HEAD] = (piece * slope[rows, c : c + HEAD]).astype(BF)
+        return carry
+
+    lax.fori_loop(0, TOK // TILE, gate_tile, 0)
+    for u in LATE:
+        terms[u] = (dot(normed_t[...], pback[:, u * WIDTH : (u + 1) * WIDTH]) * factor).astype(BF)
+        step(u, 0)
+
+    def back_tile(r, carry):
+        rows = pl.ds(pl.multiple_of(r * TILE, TILE), TILE)
         nb = nback[rows, :] + dot(pback[rows, WIDTH:], w_in_ref[:, WIDTH:], 1, 1)
         x = x_ref[rows, :].astype(F32)
         mean = jnp.mean(x, -1, keepdims=True)
@@ -293,17 +549,33 @@
         n = cent * rstd
         dn = nb * gin_ref[...]
         dx = rstd * (dn - jnp.mean(dn, -1, keepdims=True) - n * jnp.mean(dn * n, -1, keepdims=True))
-        egrad_ref[rows, :] = (dx + upstream[rows, :].astype(F32)).astype(BF)
+        egrad[rows, :] = (dx + upstream[rows, :].astype(F32)).astype(BF)
         return carry
 
     lax.fori_loop(0, TOK // TILE, back_tile, 0)
-
-    def in_columns(c, carry):
-        cols = pl.ds(pl.multiple_of(c * 256, 256), 256)
-        interm_ref[:, cols] = dot(normed_t[...], pback[:, cols]) * factor
-        return carry
-
-    lax.fori_loop(2, 8, in_columns, 0)
+    for u in LATE:
+        step(u, 1)
+
+    landed(found.at[pl.ds(0, (OWNERS - 1) * 16)], row_send)
+
+    def scatter(p, carry):
+        q = lax.rem(s + p, 8)
+        rows = pl.ds(pl.multiple_of(q * 256, 256), 256)
+        found[rows, :] = (dot(put_one[rows, :], egrad[:, :256]) + dot(put_two[rows, :], egrad[:, 256:])).astype(BF)
+        spread(found, incoming_ref, back_send, back_recv, s, t, q)
+        return carry
+
+    for n in range(4):
+        lax.fori_loop(2 * n, 2 * n + 2, scatter, 0)
+        if n < 3:
+            for u in LATE:
+                step(u, n + 2)
+    for n in range(5, 9):
+        for u in LATE:
+            step(u, n)
+    landed(incoming_ref, back_recv)
+    landed(found.at[pl.ds(0, (OWNERS - 1) * 16)], back_send)
+    landed(req_out.at[pl.ds(0, OWNERS - 1)], req_send)
 
     for h in range(HEADS):
         to = worker(h)
@@ -318,70 +590,110 @@
         left(dkv_out.at[h], dkv_send.at[h], *back)
 
 
-def layer(length, embed, out_grad, gain_in, gain_out, w_in, w_out, factor):
+    for u in range(len(ORDERS)):
+        one, two, three = ORDERS[u]
+        landed(terms.at[u, other_half], s0.at[u])
+        landed(sums_ref.at[u, half], s7.at[u])
+        for d in range(3):
+            landed(r1.at[u, d], s1.at[u, d])
+            landed(r2.at[u, d], s2.at[u, d])
+            landed(r3.at[u, d], s3.at[u, d])
+            landed(spot(u, place[one], place[two], place[three]), s4.at[u, d])
+            landed(lines(u, place[one], place[two]), s5.at[u, d])
+            landed(quarter(u, place[one]), s6.at[u, d])
+
+
+def layer_step(length, owner, item_row, item_table, out_grad, gain_in, gain_out, w_in, w_out, factor):
     vm = pl.BlockSpec(memory_space=pltpu.VMEM)
     dma = pltpu.SemaphoreType.DMA
+    n = len(ORDERS)
 
     def buf(*shape, dtype=BF):
         return pltpu.VMEM(shape, dtype)
 
+    square = buf(TOK, WIDTH)
+    wide = buf(TOK, WIDTH, dtype=F32)
+    heads, pairs, carried = buf(4, TOK, HEAD), buf(4, TOK, 2 * HEAD), buf(4, TOK + 16, HEAD)
+    message = buf(OWNERS, 1, 128, dtype=F32)
     blocks = [
-        buf(TOK, WIDTH), buf(WIDTH, TOK), buf(TOK, 4 * WIDTH, dtype=F32), buf(TOK, WIDTH), buf(TOK, WIDTH),
-        buf(TOK, WIDTH), buf(TOK, WIDTH, dtype=F32), buf(TOK, WIDTH, dtype=F32), buf(TOK, 4 * WIDTH),
-        buf(4, TOK, HEAD), buf(4, TOK, 2 * HEAD), buf(4, TOK, HEAD), buf(8, TOK, 2 * HEAD),
-        buf(4, TOK, HEAD), buf(4, TOK, HEAD), buf(4, TOK, HEAD), buf(4, TOK, HEAD),
+        square, square, buf(n, WIDTH, WIDTH), square, square, buf(TOK, 4 * WIDTH, dtype=F32), square, square,
+        square, wide, wide, buf(TOK, 4 * WIDTH),
+        heads, pairs, heads, buf(8, TOK, 2 * HEAD), carried, carried, heads, heads,
         buf(4, TOK, HEAD, dtype=F32), buf(8, TOK, 2 * HEAD, dtype=F32),
-        buf(4, TOK, 2 * HEAD), buf(4, TOK, 2 * HEAD), buf(4, TOK, HEAD), buf(4, TOK, 2 * HEAD),
-        buf(4, TOK, HEAD), buf(4, TOK, 2 * HEAD), buf(TOK, HEAD, dtype=F32),
+        pairs, pairs, heads, pairs, heads, pairs, buf(TOK, HEAD, dtype=F32),
+        message, message, buf(OWNERS * SLOTS, 128, dtype=F32), buf(ROWS, 256), buf(ROWS, 256),
+        buf(TOK, 128, dtype=jnp.int32), buf(TOK, ROWS), buf(TOK, ROWS), buf(ROWS, TOK), buf(ROWS, TOK),
+        buf(n, 256, WIDTH), buf(n, 256, WIDTH), buf(n, 3, 64, WIDTH), buf(n, 64, WIDTH),
+        buf(n, 3, 16, WIDTH), buf(n, 16, WIDTH), buf(n, 3, 16, 128),
     ]
-    sems = [dma((n,)) for n in (4, 4, 4, 8, 4, 4, 4, 4, 4, 4, 4, 4, 4, 4, 4)]
+    one, three = dma((n,)), dma((n, 3))
+    sems = [dma((c,)) for c in (4, 4, 4, 8, 4, 4, 4, 4, 4, 4, 4, 4, 4, 4, 4)]
+    sems += [dma] * 6 + [one] * 2 + [three] * 12 + [one] * 2
     return pl.pallas_call(
-        functools.partial(layer_kernel, factor),
+        functools.partial(step_kernel, factor),
         out_shape=(
             jax.ShapeDtypeStruct((TOK, WIDTH), BF),
-            jax.ShapeDtypeStruct((TOK, WIDTH), BF),
+            jax.ShapeDtypeStruct((ROWS, 256), BF),
+            jax.ShapeDtypeStruct((n, WIDTH, WIDTH), BF),
+            jax.ShapeDtypeStruct((8, OWNERS * SLOTS), F32),
+        ),
+        in_specs=[pl.BlockSpec(memory_space=pltpu.SMEM)] + [vm] * 8,
+        out_specs=(vm,) * 4,
+        scratch_shapes=blocks + sems,
+        compiler_params=pltpu.CompilerParams(
+            collective_id=0, has_side_effects=True, vmem_limit_bytes=62 * 1024 * 1024
+        ),
+    )(length, owner, item_row, item_table, out_grad, gain_in.reshape(1, -1), gain_out.reshape(1, -1), w_in, w_out)
+
+
+def finish_kernel(incoming_ref, asked_ref, sums_ref, out_ref, w_in_ref, w_out_ref, rows):
+    @pl.when(pl.program_id(0) == 0)
+    def _():
+        for q in range(8):
+            both = incoming_ref[q * 256 : (q + 1) * 256, :].astype(F32).reshape(16, 16, 256)
+            part = slice(q * 128, (q + 1) * 128)
+            rows[part, :256] = both[:, :SLOTS].reshape(128, 256).astype(BF)
+            rows[part, 256:] = both[:, SLOTS:].reshape(128, 256).astype(BF)
+
+    at = lax.broadcasted_iota(jnp.int32, (256, OWNERS * SLOTS), 0) + pl.program_id(0) * 256
+    hit = at == asked_ref[...][:1].astype(jnp.int32)
+    out_ref[...] = dot(jnp.where(hit, 1.0, 0.0).astype(BF), rows[...])
+    for u in range(4):
+        w_in_ref[:, u * WIDTH : (u + 1) * WIDTH] = sums_ref[u].astype(F32)
+    w_out_ref[...] = sums_ref[4].astype(F32)
+
+
+def finish(incoming, asked, sums):
+    n = len(ORDERS)
+    return pl.pallas_call(
+        finish_kernel,
+        grid=(8,),
+        out_shape=(
+            jax.ShapeDtypeStruct((ROWS, WIDTH), F32),
             jax.ShapeDtypeStruct((WIDTH, 4 * WIDTH), F32),
             jax.ShapeDtypeStruct((WIDTH, WIDTH), F32),
         ),
-        in_specs=[pl.BlockSpec(memory_space=pltpu.SMEM)] + [vm] * 6,
-        out_specs=(vm,) * 4,
-        scratch_shapes=blocks + sems,
-        compiler_params=pltpu.CompilerParams(
-            collective_id=0, has_side_effects=True, vmem_limit_bytes=56 * 1024 * 1024
+        in_specs=[
+            pl.BlockSpec((ROWS, 256), lambda i: (0, 0)),
+            pl.BlockSpec((8, OWNERS * SLOTS), lambda i: (0, 0)),
+            pl.BlockSpec((n, 64, WIDTH), lambda i: (0, i, 0)),
+        ],
+        out_specs=(
+            pl.BlockSpec((256, WIDTH), lambda i: (i, 0)),
+            pl.BlockSpec((64, 4 * WIDTH), lambda i: (i, 0)),
+            pl.BlockSpec((64, WIDTH), lambda i: (i, 0)),
         ),
-        cost_estimate=pl.CostEstimate(flops=14 * 10**9, bytes_accessed=12 * 2**20, transcendentals=10**7),
-    )(length, embed, out_grad, gain_in.reshape(1, -1), gain_out.reshape(1, -1), w_in, w_out)
+        scratch_shapes=[pltpu.VMEM((OWNERS * SLOTS, WIDTH), BF)],
+        compiler_params=pltpu.CompilerParams(vmem_limit_bytes=32 * 1024 * 1024),
+    )(incoming, asked, sums)
 
 
 def local(item_table, owner, item_row, lengths, gain_in, gain_out, w_in, w_out, out_grad):
-    events_here = owner.shape[1]
-    owners = lax.axis_size(("seq", "table"))
-    slots = max(2, 2 * events_here // owners)
-    width = w_out.shape[0]
-    factor = (events_here * owners) ** (-0.5)
-    target = owner[0, :, 0]
-    wanted = item_row[0]
-    chosen = (target[:, None] == jnp.arange(owners, dtype=jnp.int32)[None, :]).astype(jnp.int32)
-    before = jnp.cumsum(chosen, axis=0) - chosen
-    rank = jnp.sum(before * chosen, axis=1)
-    slot = target * slots + rank
-    request = jnp.full((owners * slots,), -1, jnp.int32).at[slot].set(wanted).reshape(owners, slots)
-    asked = lax.all_to_all(request, ("seq", "table"), split_axis=0, concat_axis=0, tiled=True)
-    found = jnp.take(item_table, jnp.maximum(asked, 0), axis=0)
-    found = jnp.where((asked >= 0)[:, :, None], found, jnp.zeros_like(found))
-    fetched = lax.all_to_all(found, ("seq", "table"), split_axis=0, concat_axis=0, tiled=True)
-    embed = jnp.take(fetched.reshape(owners * slots, width), slot, axis=0)
-    hidden, embed_grad, in_term, out_term = layer(
-        lengths, embed, out_grad[0], gain_in, gain_out, w_in, w_out, factor
+    factor = (TOK * OWNERS) ** (-0.5)
+    hidden, incoming, sums, asked = layer_step(
+        lengths, owner[0], item_row.reshape(TOK, 1), item_table, out_grad[0], gain_in, gain_out, w_in, w_out, factor
     )
-    outgoing = jnp.zeros((owners * slots, width), jnp.bfloat16).at[slot].set(embed_grad).reshape(owners, slots, width)
-    incoming = lax.all_to_all(outgoing, ("seq", "table"), split_axis=0, concat_axis=0, tiled=True)
-    table_grad = (
-        jnp.zeros((item_table.shape[0], width), jnp.float32)
-        .at[jnp.maximum(asked, 0).reshape(-1)]
-        .add(incoming.reshape(-1, width).astype(jnp.float32))
-    )
-    w_in_grad, w_out_grad = lax.psum((in_term, out_term), ("seq", "table"))
+    table_grad, w_in_grad, w_out_grad = finish(incoming, asked, sums)
     return (hidden[None], table_grad, w_in_grad, w_out_grad)
 
 

time: 345 us -> 204 us (0.59)
  waiting for transfers between devices: 163 us -> 0 us
  Pallas kernels: 88.2 us -> 195 us
  starting transfers between devices: 22.1 us -> 0 us
  blocking collectives: 20.9 us -> 0 us
  local copies, waits for them, and re-layouts: 22.3 us -> 7.58 us
  other arithmetic: 14.1 us -> 0 us
  between operations: 14.8 us -> 1.3 us
    psum x1 -> x0, waiting for transfers between devices: 124 us -> none  [local(): w_in_grad, w_out_grad = lax.psum((in_term, out_term), ('seq', 'table'))]
    pallas_call x1 -> x2, Pallas kernels: 88.2 us -> 195 us  [the longest x1 189 us: layer_step(): pl.pallas_call(functools.partial(step_kernel, factor), out_shape=(jax.Sha...]
    all_to_all x2 -> x0, waiting for transfers between devices: 38.1 us -> none  [the longest x1 19.7 us: local(): lax.all_to_all(outgoing, ('seq', 'table'), split_axis=0, concat_axis=0, t...]
    all_to_all x2 -> x0, starting transfers between devices: 22 us -> none  [the longest x1 17.5 us: local(): lax.all_to_all(outgoing, ('seq', 'table'), split_axis=0, concat_axis=0, t...]
    all_to_all x1 -> x0, blocking collectives: 20.9 us -> none  [local(): lax.all_to_all(request, ('seq', 'table'), split_axis=0, concat_axis=0, ti...]
    scatter-add x1 -> x0, other arithmetic: 8.95 us -> none  [local(): table_grad = jnp.zeros((item_table.shape[0], width), jnp.float32).at[jnp....]
    gather x2 -> x0, local copies, waits for them, and re-layouts: 6.58 us -> none  [the longest x1 3.97 us: local(): found = jnp.take(item_table, jnp.maximum(asked, 0), axis=0)]
    scatter x2 -> x0, local copies, waits for them, and re-layouts: 6.55 us -> none  [the longest x1 3.95 us: local(): jnp.zeros((owners * slots, width), jnp.bfloat16).at[slot].set(embed_grad)]
  transfers between devices with their start and end apart: 3 -> 0, of which waited for: 3 -> 0; matrix products, arithmetic and copies ran while one was open for 4% -> 0% of each run, Pallas kernels for 0% -> 0%
where the time goes in v3:
time: 204 us
  Pallas kernels  195 us (96%)
  local copies, waits for them, and re-layouts  7.58 us (4%)
    pallas_call x1, Pallas kernels, layer_step(): pl.pallas_call(functools.partial(step_kernel, factor), out_shape=(jax.Sha...  189 us
    pallas_call x1, Pallas kernels, finish(): pl.pallas_call(finish_kernel, grid=(8,), out_shape=(jax.ShapeDtypeStruct(...  6.21 us
    unnamed x9, local copies, waits for them, and re-layouts  4.51 us

profile of v3, /device:TPU:1, one launch (start us, length us, event | category | flops | bytes accessed | tf_op | source)
XLA Modules:
  0.0 204.1 jit_solution(6527171239665315569)
XLA Ops:
  1.3 1.5 copy.13.owner_ref
  2.8 1.5 copy.14.row_ref
  4.3 189.1 %shard_map.120 = (bf16[512,512]{1,0:T(8,128)(2,1)}, bf16[2048,256]{1,0:T(8,128)(2,1)}, bf16[5,512,512]{2,1,0:T(8,128)(2,1)}, f32[8,1024]{1,0:T(8,128)}) custom-call(s32[1]{0:T(128)S(6)} %copy.16.len_ref, s32[512,1]{1,0:T(8,128)} %copy.13.owner_ref, s32[512,1]{1,0:T(8,128)} %copy.14.row_ref, bf16[2048,512]{1,0:T(8,128)(2,1)} %table_ref.1, ...), custom_call_target="tpu_custom_call" | custom-call | tf_op jit(solution)/shard_map/pallas_call | solution.py:632
  193.4 0.0 copy-start
  193.4 1.7 copy-done
  195.2 0.0 copy-start.1
  195.2 1.2 copy-done.1
  196.4 0.0 copy-start.2
  196.4 0.8 copy-done.2
  197.1 0.0 copy-start.3
  197.1 6.2 %shard_map.121 = (f32[2048,512]{1,0:T(8,128)}, f32[512,2048]{1,0:T(8,128)}, f32[512,512]{1,0:T(8,128)}) custom-call(bf16[2048,256]{1,0:T(8,128)(2,1)S(1)} %copy-done.1, f32[8,1024]{1,0:T(8,128)S(1)} %copy-done.2, bf16[5,512,512]{2,1,0:T(8,128)(2,1)S(1)} %copy-done), custom_call_target="tpu_custom_call" | custom-call | tf_op jit(solution)/shard_map/pallas_call | solution.py:668
  203.3 0.0 copy-done.3
  203.4 0.8 copy.17
Async XLA Ops:
  193.4 1.7 copy-start
  195.2 1.2 copy-start.1
  196.4 0.8 copy-start.2
  197.1 6.2 %copy-start.3 = (bf16[512,512]{1,0:T(8,128)(2,1)S(1)}, bf16[512,512]{1,0:T(8,128)(2,1)}, u32[]{:S(2)}) copy-start(bf16[512,512]{1,0:T(8,128)(2,1)} %get-tuple-element.11) | copy-start | bytes 1572868

commit v4 on v3

--- a/solution.py
+++ b/solution.py
@@ -82,16 +82,16 @@
 
 def step_kernel(
     factor,
-    len_ref, owner_ref, row_ref, table_ref, og_ref, gin_ref, gout_ref, w_in_ref, w_out_ref,
+    len_ref, owner_ref, row_ref, table_hbm, og_hbm, gin_ref, gout_ref, w_in_hbm, w_out_hbm,
     hidden_ref, incoming_ref, sums_ref, asked_ref,
-    x_ref, egrad, terms, normed, normed_t, slope, gate, upstream, joined, jgrad, nback, pback,
+    table_ref, og_ref, w_in_ref, w_out_ref, x_ref, egrad, terms, normed, normed_t, slope, gate, upstream, joined, jgrad, nback, pback,
     q_out, kv_out, q_in, kv_in, mix_out, mix_in, dm_out, dm_in,
     dq_acc, dkv_acc, part_out, part_in, dq_out, dkv_out, dq_in, dkv_in, m_acc,
     req_out, req_in, asked_col, found, fetched, spot_col, pick_one, pick_two, put_one, put_two,
     r0, a1, r1, a2, r2, a3, r3,
     q_send, q_recv, kv_send, kv_recv, fwd_send, mix_send, mix_recv, dm_send, dm_recv,
     part_send, part_recv, dq_send, dq_recv, dkv_send, dkv_recv,
-    req_send, req_recv, row_send, row_recv, back_send, back_recv,
+    load_sem, req_send, req_recv, row_send, row_recv, back_send, back_recv,
     s0, v0, s1, v1, s2, v2, s3, v3, s4, v4, s5, v5, s6, v6, s7, v7,
 ):
     s = lax.axis_index("seq")
@@ -100,7 +100,8 @@
     core = lax.rem(t, 2)
     base = t - core
     head = lax.rem(s, HEADS)
-    user_core = s // HEADS
+    user_core = lax.rem(lax.rem(s, HEADS) + s // HEADS, 2)
+    upward = user_core == 1
     sibling = base + 1 - core
     part_of_s = lax.rem((s + 1) // 2, 2)
     slot_of_s = s // 2
@@ -128,7 +129,7 @@
             landed(src, send)
 
     def worker(h):
-        return core * HEADS + h, base + part_of_s
+        return lax.rem(core + h, 2) * HEADS + h, base + part_of_s
 
     def mine_of(k):
         return 2 * k + lax.rem(k + core, 2)
@@ -240,21 +241,29 @@
         else:
             landed(sums_ref.at[u, other_half], v7.at[u])
 
+    copies = [
+        pltpu.make_async_copy(src, dst, load_sem.at[n])
+        for n, (src, dst) in enumerate(
+            ((table_hbm, table_ref), (og_hbm, og_ref), (w_out_hbm, w_out_ref), (w_in_hbm, w_in_ref))
+        )
+    ]
+    for copy in copies:
+        copy.start()
+
     target = owner_ref[...]
-    lane = lax.broadcasted_iota(jnp.int32, (TOK, OWNERS), 1)
-    chosen_mask = lane == target
+    line_e = lax.broadcasted_iota(jnp.int32, (OWNERS, TOK), 0)
+    chosen_mask = line_e == target
     chosen = jnp.where(chosen_mask, 1.0, 0.0).astype(BF)
-    below = jnp.where(
-        lax.broadcasted_iota(jnp.int32, (TOK, TOK), 1) < lax.broadcasted_iota(jnp.int32, (TOK, TOK), 0), 1.0, 0.0
+    above = jnp.where(
+        lax.broadcasted_iota(jnp.int32, (TOK, TOK), 0) < lax.broadcasted_iota(jnp.int32, (TOK, TOK), 1), 1.0, 0.0
     ).astype(BF)
-    before = dot(below, chosen)
-    rank = jnp.sum(jnp.where(chosen_mask, before, 0.0), axis=1, keepdims=True).astype(jnp.int32)
+    before = dot(chosen, above)
+    rank = jnp.sum(jnp.where(chosen_mask, before, 0.0), axis=0, keepdims=True).astype(jnp.int32)
     value = row_ref[...] + 1
     high = (value >> 7).astype(F32)
     low = (value & 127).astype(F32)
-    message = jnp.where(lane == rank, high, 0.0) + jnp.where(lane == rank + SLOTS, low, 0.0)
-    req_out[:, 0, :] = dot(chosen, message.astype(BF), 0, 0)
-
+    message = jnp.where(line_e == rank, high, 0.0) + jnp.where(line_e == rank + SLOTS, low, 0.0)
+    req_out[:, 0, :] = dot(chosen, message.astype(BF), 1, 1)
     pl.semaphore_wait(barrier, OWNERS - 1)
 
     def ask(p, carry):
@@ -266,9 +275,11 @@
 
     lax.fori_loop(0, OWNERS, ask, 0)
 
-    spot_of = target * 16 + rank
-    slot_row = jnp.broadcast_to(spot_of.astype(F32), (TOK, 128)).T[:1].astype(jnp.int32)
+    slot_row = target * 16 + rank
+    spot_col[...] = jnp.broadcast_to(slot_row.astype(F32), (128, TOK)).T.astype(jnp.int32)
     live = live_rows(0, TOK)
+    copies[1].wait()
+    copies[2].wait()
     upstream[...] = (og_ref[...].astype(F32) * live).astype(BF)
     jgrad[...] = dot(upstream[...], w_out_ref[...], 1, 1)
     number = lax.broadcasted_iota(jnp.int32, (OWNERS * SLOTS, OWNERS), 0)
@@ -289,6 +300,8 @@
     asked_col[...] = wide
     asked_ref[...] = wide.T[:8]
 
+    copies[0].wait()
+
     def gather(p, carry):
         q = lax.rem(s + p, 8)
         column = asked_col[pl.ds(pl.multiple_of(q * 128, 128), 128), :][:, :1].astype(jnp.int32)
@@ -310,10 +323,10 @@
         pick_two[rows, :] = jnp.where(at == spots + SLOTS, 1.0, 0.0).astype(BF)
         return carry
 
-    spot_col[...] = jnp.broadcast_to(spot_of, (TOK, 128))
     lax.fori_loop(0, TOK // TILE, pick_tile, 0)
     dq_acc[...] = jnp.zeros_like(dq_acc)
     dkv_acc[...] = jnp.zeros_like(dkv_acc)
+    copies[3].wait()
     landed(fetched, row_recv)
 
     def norm_tile(r, carry):
@@ -465,55 +478,77 @@
         dkv_acc[j, :, :HEAD] += dot(sb, q)
         dq_acc[k] += dot(sb, kv_in[j, :, :HEAD], 0, 0)
 
-    def finish(m):
-        d = mine_of(m)
-        landed(part_in.at[m], part_recv.at[m])
-        total = dkv_acc[d] + part_in[m].astype(F32)
-        dkv_out[m, :, :HEAD] = (total[:, :HEAD] * SCALE).astype(BF)
-        dkv_out[m, :, HEAD:] = total[:, HEAD:].astype(BF)
-        push(dkv_out.at[m], dkv_in.at[head], dkv_send.at[m], dkv_recv.at[head], d, base + user_core)
-
-    def backward(m, carry):
+    def send_back(out, into, send, recv, k):
+        push(out.at[k], into.at[head], send.at[k], recv.at[head], mine_of(k), base + user_core)
+
+    def finish_query(k):
+        dq_out[k] = (dq_acc[k] * SCALE).astype(BF)
+        send_back(dq_out, dq_in, dq_send, dq_recv, k)
+
+    def finish_key(j):
+        m = j // 2
+
+        @pl.when(mine_of(m) == j)
+        def _():
+            landed(part_in.at[m], part_recv.at[m])
+            total = dkv_acc[j] + part_in[m].astype(F32)
+            dkv_out[m, :, :HEAD] = (total[:, :HEAD] * SCALE).astype(BF)
+            dkv_out[m, :, HEAD:] = total[:, HEAD:].astype(BF)
+            send_back(dkv_out, dkv_in, dkv_send, dkv_recv, m)
+
+    def key_block(n):
+        return jnp.where(upward, n, 7 - n)
+
+    def backward(n, carry):
+        j = key_block(n)
+        m = j // 2
         i = mine_of(m)
 
-        def one(jj, c):
-            j = 2 * m + jj
-
-            @pl.when(i == j)
+        @pl.when(i == j)
+        def _():
+            backward_pair(m, j, True)
+
+        def inner(k, c):
+            backward_pair(k, j, False)
+            return c
+
+        lax.fori_loop(jnp.where(i > j, m, m + 1), 4, inner, 0)
+
+        @pl.when(i != j)
+        def _():
+            part_out[m] = dkv_acc[j].astype(BF)
+            pltpu.make_async_remote_copy(
+                src_ref=part_out.at[m], dst_ref=part_in.at[m], send_sem=part_send.at[m], recv_sem=part_recv.at[m],
+                device_id=(s, sibling), device_id_type=MESH,
+            ).start()
+
+        @pl.when(jnp.logical_and(i == j, upward))
+        def _():
+            finish_query(m)
+
+        @pl.when(n > 0)
+        def _():
+            finish_key(key_block(n - 1))
+
+        for e in range(4):
+
+            @pl.when(n == jnp.where(upward, e, e + 3))
             def _():
-                backward_pair(m, j, True)
-
-            def inner(k, cc):
-                backward_pair(k, j, False)
-                return cc
-
-            lax.fori_loop(jnp.where(i > j, m, m + 1), 4, inner, 0)
-            for n in range(8):
-
-                @pl.when(j == n)
-                def _():
-                    for u in EARLY:
-                        step(u, n + 1)
-
-            return c
-
-        lax.fori_loop(0, 2, one, 0)
-        part_out[m] = dkv_acc[other_of(m)].astype(BF)
-        pltpu.make_async_remote_copy(
-            src_ref=part_out.at[m], dst_ref=part_in.at[m], send_sem=part_send.at[m], recv_sem=part_recv.at[m],
-            device_id=(s, sibling), device_id_type=MESH,
-        ).start()
-        dq_out[m] = (dq_acc[m] * SCALE).astype(BF)
-        push(dq_out.at[m], dq_in.at[head], dq_send.at[m], dq_recv.at[head], i, base + user_core)
-
-        @pl.when(m > 0)
-        def _():
-            finish(m - 1)
-
-        return carry
-
-    lax.fori_loop(0, 4, backward, 0)
-    finish(3)
+                for u in EARLY:
+                    step(u, e + 1)
+
+        return carry
+
+    lax.fori_loop(0, 8, backward, 0)
+
+    @pl.when(jnp.logical_not(upward))
+    def _():
+        for k in range(4):
+            finish_query(k)
+
+    finish_key(key_block(7))
+    for u in EARLY:
+        step(u, 5)
 
     for h in range(HEADS):
         landed(dq_in.at[h], dq_recv.at[h])
@@ -537,6 +572,8 @@
     for u in LATE:
         terms[u] = (dot(normed_t[...], pback[:, u * WIDTH : (u + 1) * WIDTH]) * factor).astype(BF)
         step(u, 0)
+    for u in EARLY:
+        step(u, 6)
 
     def back_tile(r, carry):
         rows = pl.ds(pl.multiple_of(r * TILE, TILE), TILE)
@@ -555,6 +592,8 @@
     lax.fori_loop(0, TOK // TILE, back_tile, 0)
     for u in LATE:
         step(u, 1)
+    for u in EARLY:
+        step(u, 7)
 
     landed(found.at[pl.ds(0, (OWNERS - 1) * 16)], row_send)
 
@@ -570,6 +609,9 @@
         if n < 3:
             for u in LATE:
                 step(u, n + 2)
+        if n == 1:
+            for u in EARLY:
+                step(u, 8)
     for n in range(5, 9):
         for u in LATE:
             step(u, n)
@@ -604,7 +646,7 @@
 
 
 def layer_step(length, owner, item_row, item_table, out_grad, gain_in, gain_out, w_in, w_out, factor):
-    vm = pl.BlockSpec(memory_space=pltpu.VMEM)
+    vm, far = pl.BlockSpec(memory_space=pltpu.VMEM), pl.BlockSpec(memory_space=pl.ANY)
     dma = pltpu.SemaphoreType.DMA
     n = len(ORDERS)
 
@@ -616,6 +658,7 @@
     heads, pairs, carried = buf(4, TOK, HEAD), buf(4, TOK, 2 * HEAD), buf(4, TOK + 16, HEAD)
     message = buf(OWNERS, 1, 128, dtype=F32)
     blocks = [
+        buf(ROWS, WIDTH), square, buf(WIDTH, 4 * WIDTH), square,
         square, square, buf(n, WIDTH, WIDTH), square, square, buf(TOK, 4 * WIDTH, dtype=F32), square, square,
         square, wide, wide, buf(TOK, 4 * WIDTH),
         heads, pairs, heads, buf(8, TOK, 2 * HEAD), carried, carried, heads, heads,
@@ -628,7 +671,7 @@
     ]
     one, three = dma((n,)), dma((n, 3))
     sems = [dma((c,)) for c in (4, 4, 4, 8, 4, 4, 4, 4, 4, 4, 4, 4, 4, 4, 4)]
-    sems += [dma] * 6 + [one] * 2 + [three] * 12 + [one] * 2
+    sems += [dma((4,))] + [dma] * 6 + [one] * 2 + [three] * 12 + [one] * 2
     return pl.pallas_call(
         functools.partial(step_kernel, factor),
         out_shape=(
@@ -637,7 +680,7 @@
             jax.ShapeDtypeStruct((n, WIDTH, WIDTH), BF),
             jax.ShapeDtypeStruct((8, OWNERS * SLOTS), F32),
         ),
-        in_specs=[pl.BlockSpec(memory_space=pltpu.SMEM)] + [vm] * 8,
+        in_specs=[pl.BlockSpec(memory_space=pltpu.SMEM), vm, vm, far, far, vm, vm, far, far],
         out_specs=(vm,) * 4,
         scratch_shapes=blocks + sems,
         compiler_params=pltpu.CompilerParams(
@@ -684,14 +727,14 @@
             pl.BlockSpec((64, WIDTH), lambda i: (i, 0)),
         ),
         scratch_shapes=[pltpu.VMEM((OWNERS * SLOTS, WIDTH), BF)],
-        compiler_params=pltpu.CompilerParams(vmem_limit_bytes=32 * 1024 * 1024),
+        compiler_params=pltpu.CompilerParams(vmem_limit_bytes=60 * 1024 * 1024),
     )(incoming, asked, sums)
 
 
 def local(item_table, owner, item_row, lengths, gain_in, gain_out, w_in, w_out, out_grad):
     factor = (TOK * OWNERS) ** (-0.5)
     hidden, incoming, sums, asked = layer_step(
-        lengths, owner[0], item_row.reshape(TOK, 1), item_table, out_grad[0], gain_in, gain_out, w_in, w_out, factor
+        lengths, owner.reshape(1, TOK), item_row, item_table, out_grad[0], gain_in, gain_out, w_in, w_out, factor
     )
     table_grad, w_in_grad, w_out_grad = finish(incoming, asked, sums)
     return (hidden[None], table_grad, w_in_grad, w_out_grad)

time: 204 us -> 186 us (0.912)
  Pallas kernels: 195 us -> 183 us
  local copies, waits for them, and re-layouts: 7.58 us -> 0.8 us
    pallas_call x1, Pallas kernels: 189 us -> 175 us  [layer_step(): pl.pallas_call(functools.partial(step_kernel, factor), out_shape=(jax.Sha...]
    unnamed x9 -> x3, local copies, waits for them, and re-layouts: 4.51 us -> 0.8 us
    pallas_call x1, Pallas kernels: 6.21 us -> 8.85 us  [finish(): pl.pallas_call(finish_kernel, grid=(8,), out_shape=(jax.ShapeDtypeStruct(...]
where the time goes in v4:
time: 186 us
  Pallas kernels  183 us (98%)
    pallas_call x1, Pallas kernels, layer_step(): pl.pallas_call(functools.partial(step_kernel, factor), out_shape=(jax.Sha...  175 us
    pallas_call x1, Pallas kernels, finish(): pl.pallas_call(finish_kernel, grid=(8,), out_shape=(jax.ShapeDtypeStruct(...  8.85 us

profile of v4, /device:TPU:1, one launch (start us, length us, event | category | flops | bytes accessed | tf_op | source)
XLA Modules:
  0.0 185.5 jit_solution(14977735877190199431)
XLA Ops:
  1.3 174.6 %shard_map.120 = (bf16[512,512]{1,0:T(8,128)(2,1)}, bf16[2048,256]{1,0:T(8,128)(2,1)}, bf16[5,512,512]{2,1,0:T(8,128)(2,1)}, f32[8,1024]{1,0:T(8,128)}) custom-call(s32[1]{0:T(128)S(6)} %copy.14.len_ref, s32[1,512]{1,0:T(1,128)} %bitcast.7, s32[1,512]{1,0:T(1,128)} %row_ref.1, bf16[2048,512]{1,0:T(8,128)(2,1)} %table_hbm.1, bf16[512,512]{1,0:T(8,128)(2,1)} %bitcast.6, ...), custom_call_target="tpu_custom_call" | custom-call | tf_op jit(solution)/shard_map/pallas_call | solution.py:675
  175.9 0.0 copy-start
  175.9 8.8 %shard_map.121 = (f32[2048,512]{1,0:T(8,128)}, f32[512,2048]{1,0:T(8,128)}, f32[512,512]{1,0:T(8,128)}) custom-call(bf16[2048,256]{1,0:T(8,128)(2,1)} %get-tuple-element.12.incoming_ref, f32[8,1024]{1,0:T(8,128)} %get-tuple-element.13.asked_ref, bf16[5,512,512]{2,1,0:T(8,128)(2,1)} %get-tuple-element.14.sums_ref), custom_call_target="tpu_custom_call" | custom-call | tf_op jit(solution)/shard_map/pallas_call | solution.py:711
  184.7 0.0 copy-done
  184.7 0.8 copy.15
Async XLA Ops:
  175.9 8.9 %copy-start = (bf16[512,512]{1,0:T(8,128)(2,1)S(1)}, bf16[512,512]{1,0:T(8,128)(2,1)}, u32[]{:S(2)}) copy-start(bf16[512,512]{1,0:T(8,128)(2,1)} %get-tuple-element.11) | copy-start | bytes 1572868

commit v5 on v4

--- a/solution.py
+++ b/solution.py
@@ -459,6 +459,8 @@
         step(u, 0)
     hidden_ref[...] = ((dot(joined[...], w_out_ref[...]) + x_ref[...].astype(F32)) * live).astype(BF)
     nback[...] = dot(pback[:, :WIDTH], w_in_ref[:, :WIDTH], 1, 1)
+    for u in EARLY:
+        step(u, 1)
 
     for k in range(4):
         landed(dm_in.at[k], dm_recv.at[k])
@@ -530,13 +532,6 @@
         def _():
             finish_key(key_block(n - 1))
 
-        for e in range(4):
-
-            @pl.when(n == jnp.where(upward, e, e + 3))
-            def _():
-                for u in EARLY:
-                    step(u, e + 1)
-
         return carry
 
     lax.fori_loop(0, 8, backward, 0)
@@ -548,7 +543,7 @@
 
     finish_key(key_block(7))
     for u in EARLY:
-        step(u, 5)
+        step(u, 2)
 
     for h in range(HEADS):
         landed(dq_in.at[h], dq_recv.at[h])
@@ -573,7 +568,7 @@
         terms[u] = (dot(normed_t[...], pback[:, u * WIDTH : (u + 1) * WIDTH]) * factor).astype(BF)
         step(u, 0)
     for u in EARLY:
-        step(u, 6)
+        step(u, 3)
 
     def back_tile(r, carry):
         rows = pl.ds(pl.multiple_of(r * TILE, TILE), TILE)
@@ -593,7 +588,7 @@
     for u in LATE:
         step(u, 1)
     for u in EARLY:
-        step(u, 7)
+        step(u, 4)
 
     landed(found.at[pl.ds(0, (OWNERS - 1) * 16)], row_send)
 
@@ -609,12 +604,14 @@
         if n < 3:
             for u in LATE:
                 step(u, n + 2)
-        if n == 1:
             for u in EARLY:
-                step(u, 8)
+                step(u, n + 5)
     for n in range(5, 9):
         for u in LATE:
             step(u, n)
+        if n == 5:
+            for u in EARLY:
+                step(u, 8)
     landed(incoming_ref, back_recv)
     landed(found.at[pl.ds(0, (OWNERS - 1) * 16)], back_send)
     landed(req_out.at[pl.ds(0, OWNERS - 1)], req_send)

time: 186 us -> 181 us (0.973)
  Pallas kernels: 183 us -> 179 us
    pallas_call x1, Pallas kernels: 175 us -> 170 us  [layer_step(): pl.pallas_call(functools.partial(step_kernel, factor), out_shape=(jax.Sha...]
where the time goes in v5:
time: 181 us
  Pallas kernels  179 us (99%)
    pallas_call x1, Pallas kernels, layer_step(): pl.pallas_call(functools.partial(step_kernel, factor), out_shape=(jax.Sha...  170 us
    pallas_call x1, Pallas kernels, finish(): pl.pallas_call(finish_kernel, grid=(8,), out_shape=(jax.ShapeDtypeStruct(...  8.86 us

profile of v5, /device:TPU:1, one launch (start us, length us, event | category | flops | bytes accessed | tf_op | source)
XLA Modules:
  0.0 180.7 jit_solution(7458373650932785206)
XLA Ops:
  1.3 169.8 %shard_map.120 = (bf16[512,512]{1,0:T(8,128)(2,1)}, bf16[2048,256]{1,0:T(8,128)(2,1)}, bf16[5,512,512]{2,1,0:T(8,128)(2,1)}, f32[8,1024]{1,0:T(8,128)}) custom-call(s32[1]{0:T(128)S(6)} %copy.14.len_ref, s32[1,512]{1,0:T(1,128)} %bitcast.7, s32[1,512]{1,0:T(1,128)} %row_ref.1, bf16[2048,512]{1,0:T(8,128)(2,1)} %table_hbm.1, bf16[512,512]{1,0:T(8,128)(2,1)} %bitcast.6, ...), custom_call_target="tpu_custom_call" | custom-call | tf_op jit(solution)/shard_map/pallas_call | solution.py:672
  171.1 0.0 copy-start
  171.1 8.9 %shard_map.121 = (f32[2048,512]{1,0:T(8,128)}, f32[512,2048]{1,0:T(8,128)}, f32[512,512]{1,0:T(8,128)}) custom-call(bf16[2048,256]{1,0:T(8,128)(2,1)} %get-tuple-element.12.incoming_ref, f32[8,1024]{1,0:T(8,128)} %get-tuple-element.13.asked_ref, bf16[5,512,512]{2,1,0:T(8,128)(2,1)} %get-tuple-element.14.sums_ref), custom_call_target="tpu_custom_call" | custom-call | tf_op jit(solution)/shard_map/pallas_call | solution.py:708
  179.9 0.0 copy-done
  179.9 0.8 copy.15
Async XLA Ops:
  171.1 8.9 %copy-start = (bf16[512,512]{1,0:T(8,128)(2,1)S(1)}, bf16[512,512]{1,0:T(8,128)(2,1)}, u32[]{:S(2)}) copy-start(bf16[512,512]{1,0:T(8,128)(2,1)} %get-tuple-element.11) | copy-start | bytes 1572868

commit v6 on v5

--- a/solution.py
+++ b/solution.py
@@ -66,13 +66,14 @@
     return pl.ds(pl.multiple_of(index * 16, 16), 16)
 
 
-def spread(src, dst, send, recv, s, t, to_s):
-    def one(p, carry):
+def spread(src, dst, send, recv, s, t, to_s, part):
+    send_rows(src, dst, send, recv, s, t, to_s, t, part(to_s * 16 + t), part(s * 16 + t))
+    for p in range(1, 16):
         to_t = lax.rem(t + p, 16)
-        send_rows(src, dst, send, recv, s, t, to_s, to_t, sixteen(to_s * 16 + to_t), sixteen(s * 16 + t))
-        return carry
-
-    lax.fori_loop(0, 16, one, 0)
+        pltpu.make_async_remote_copy(
+            src_ref=src.at[part(to_s * 16 + to_t)], dst_ref=dst.at[part(s * 16 + t)], send_sem=send, recv_sem=recv,
+            device_id=(to_s, to_t), device_id_type=MESH,
+        ).start()
 
 
 ORDERS = ("zxy", "xyz", "yzx", "zxy", "zyx")
@@ -267,13 +268,10 @@
     pl.semaphore_wait(barrier, OWNERS - 1)
 
     def ask(p, carry):
-        other = lax.rem(me + p, OWNERS)
-        send_rows(
-            req_out, req_in, req_send, req_recv, s, t, other // 16, lax.rem(other, 16), other, me
-        )
-        return carry
-
-    lax.fori_loop(0, OWNERS, ask, 0)
+        spread(req_out, req_in, req_send, req_recv, s, t, lax.rem(s + p, 8), lambda index: index)
+        return carry
+
+    lax.fori_loop(0, 8, ask, 0)
 
     slot_row = target * 16 + rank
     spot_col[...] = jnp.broadcast_to(slot_row.astype(F32), (128, TOK)).T.astype(jnp.int32)
@@ -311,7 +309,7 @@
             [rows[:, :256].reshape(16, SLOTS, 256), rows[:, 256:].reshape(16, SLOTS, 256)], axis=1
         )
         found[pl.ds(pl.multiple_of(q * 256, 256), 256), :] = both.reshape(256, 256).astype(BF)
-        spread(found, fetched, row_send, row_recv, s, t, q)
+        spread(found, fetched, row_send, row_recv, s, t, q, sixteen)
         return carry
 
     lax.fori_loop(0, 8, gather, 0)
@@ -349,12 +347,14 @@
         slope[:, pl.ds(first, columns)] = 0.5 * (1.0 + th) * (1.0 + half - half * th)
         return half + half * th
 
-    for h in range(HEADS):
-        kv_out[h, :, :HEAD] = project(3 * WIDTH + h * HEAD, HEAD).astype(BF)
-        kv_out[h, :, HEAD:] = (project(WIDTH + h * HEAD, HEAD) * live).astype(BF)
+    far_first = [lax.rem(cx + d, HEADS) for d in (2, 1, 3, 0)]
+    for h in far_first:
+        column = pl.multiple_of(h * HEAD, HEAD)
+        kv_out[h, :, :HEAD] = project(3 * WIDTH + column, HEAD).astype(BF)
+        kv_out[h, :, HEAD:] = (project(WIDTH + column, HEAD) * live).astype(BF)
         to = worker(h)
         push(kv_out.at[h], kv_in.at[s], kv_send.at[h], kv_recv.at[s], *to)
-        q_out[h] = project(2 * WIDTH + h * HEAD, HEAD).astype(BF)
+        q_out[h] = project(2 * WIDTH + column, HEAD).astype(BF)
         push(q_out.at[h], q_in.at[slot_of_s], q_send.at[h], q_recv.at[slot_of_s], *to)
 
     gate[:, :256] = project(0, 256).astype(BF)
@@ -450,7 +450,7 @@
         return carry
 
     lax.fori_loop(0, TOK // TILE, post_tile, 0)
-    for h in range(HEADS):
+    for h in far_first:
         push(dm_out.at[h], dm_in.at[slot_of_s], dm_send.at[h], dm_recv.at[slot_of_s], *worker(h))
 
     terms[4] = (dot(joined[...], upstream[...], 0, 0) * factor).astype(BF)
@@ -584,11 +584,16 @@
         egrad[rows, :] = (dx + upstream[rows, :].astype(F32)).astype(BF)
         return carry
 
-    lax.fori_loop(0, TOK // TILE, back_tile, 0)
+    lax.fori_loop(0, 2, back_tile, 0)
     for u in LATE:
         step(u, 1)
     for u in EARLY:
         step(u, 4)
+    lax.fori_loop(2, 4, back_tile, 0)
+    for u in LATE:
+        step(u, 2)
+    for u in EARLY:
+        step(u, 5)
 
     landed(found.at[pl.ds(0, (OWNERS - 1) * 16)], row_send)
 
@@ -596,22 +601,19 @@
         q = lax.rem(s + p, 8)
         rows = pl.ds(pl.multiple_of(q * 256, 256), 256)
         found[rows, :] = (dot(put_one[rows, :], egrad[:, :256]) + dot(put_two[rows, :], egrad[:, 256:])).astype(BF)
-        spread(found, incoming_ref, back_send, back_recv, s, t, q)
+        spread(found, incoming_ref, back_send, back_recv, s, t, q, sixteen)
         return carry
 
     for n in range(4):
         lax.fori_loop(2 * n, 2 * n + 2, scatter, 0)
+        for u in LATE:
+            step(u, n + 3)
         if n < 3:
-            for u in LATE:
-                step(u, n + 2)
             for u in EARLY:
-                step(u, n + 5)
-    for n in range(5, 9):
+                step(u, n + 6)
+    for n in range(7, 9):
         for u in LATE:
             step(u, n)
-        if n == 5:
-            for u in EARLY:
-                step(u, 8)
     landed(incoming_ref, back_recv)
     landed(found.at[pl.ds(0, (OWNERS - 1) * 16)], back_send)
     landed(req_out.at[pl.ds(0, OWNERS - 1)], req_send)

time: 181 us -> 177 us (0.978)
  Pallas kernels: 179 us -> 174 us
    pallas_call x1, Pallas kernels: 170 us -> 165 us  [layer_step(): pl.pallas_call(functools.partial(step_kernel, factor), out_shape=(jax.Sha...]
where the time goes in v6:
time: 177 us; the launch traced here: 176 us
  Pallas kernels  174 us (98%)
    pallas_call x1, Pallas kernels, layer_step(): pl.pallas_call(functools.partial(step_kernel, factor), out_shape=(jax.Sha...  165 us
    pallas_call x1, Pallas kernels, finish(): pl.pallas_call(finish_kernel, grid=(8,), out_shape=(jax.ShapeDtypeStruct(...  8.85 us

profile of v6, /device:TPU:1, one launch (start us, length us, event | category | flops | bytes accessed | tf_op | source)
XLA Modules:
  0.0 176.4 jit_solution(11986543973833258940)
XLA Ops:
  1.3 165.5 %shard_map.120 = (bf16[512,512]{1,0:T(8,128)(2,1)}, bf16[2048,256]{1,0:T(8,128)(2,1)}, bf16[5,512,512]{2,1,0:T(8,128)(2,1)}, f32[8,1024]{1,0:T(8,128)}) custom-call(s32[1]{0:T(128)S(6)} %copy.14.len_ref, s32[1,512]{1,0:T(1,128)} %bitcast.7, s32[1,512]{1,0:T(1,128)} %row_ref.1, bf16[2048,512]{1,0:T(8,128)(2,1)} %table_hbm.1, bf16[512,512]{1,0:T(8,128)(2,1)} %bitcast.6, ...), custom_call_target="tpu_custom_call" | custom-call | tf_op jit(solution)/shard_map/pallas_call | solution.py:674
  166.8 0.0 copy-start
  166.8 8.8 %shard_map.121 = (f32[2048,512]{1,0:T(8,128)}, f32[512,2048]{1,0:T(8,128)}, f32[512,512]{1,0:T(8,128)}) custom-call(bf16[2048,256]{1,0:T(8,128)(2,1)} %get-tuple-element.12.incoming_ref, f32[8,1024]{1,0:T(8,128)} %get-tuple-element.13.asked_ref, bf16[5,512,512]{2,1,0:T(8,128)(2,1)} %get-tuple-element.14.sums_ref), custom_call_target="tpu_custom_call" | custom-call | tf_op jit(solution)/shard_map/pallas_call | solution.py:710
  175.6 0.0 copy-done
  175.6 0.8 copy.15
Async XLA Ops:
  166.8 8.9 %copy-start = (bf16[512,512]{1,0:T(8,128)(2,1)S(1)}, bf16[512,512]{1,0:T(8,128)(2,1)}, u32[]{:S(2)}) copy-start(bf16[512,512]{1,0:T(8,128)(2,1)} %get-tuple-element.11) | copy-start | bytes 1572868

commit v7 on v6

--- a/solution.py
+++ b/solution.py
@@ -84,8 +84,8 @@
 def step_kernel(
     factor,
     len_ref, owner_ref, row_ref, table_hbm, og_hbm, gin_ref, gout_ref, w_in_hbm, w_out_hbm,
-    hidden_ref, incoming_ref, sums_ref, asked_ref,
-    table_ref, og_ref, w_in_ref, w_out_ref, x_ref, egrad, terms, normed, normed_t, slope, gate, upstream, joined, jgrad, nback, pback,
+    hidden_ref, rows_ref, sums_ref, asked_ref,
+    table_ref, og_ref, w_in_ref, w_out_ref, incoming, x_ref, egrad, terms, normed, normed_t, slope, gate, upstream, joined, jgrad, nback, pback,
     q_out, kv_out, q_in, kv_in, mix_out, mix_in, dm_out, dm_in,
     dq_acc, dkv_acc, part_out, part_in, dq_out, dkv_out, dq_in, dkv_in, m_acc,
     req_out, req_in, asked_col, found, fetched, spot_col, pick_one, pick_two, put_one, put_two,
@@ -388,18 +388,28 @@
             w = jnp.where(col <= row, w, 0.0)
         return dot(w.astype(BF), kv_in[j, :, HEAD:])
 
-    take(0)
-
-    def forward(k, carry):
-        i = mine_of(k)
-
-        @pl.when(k < 3)
-        def _():
-            take(k + 1)
-
+    def take_one(k, carry):
+        take(k)
+        return carry
+
+    lax.fori_loop(0, jnp.where(upward, 1, 4), take_one, 0)
+
+    def arrive(k, carry):
         landed(q_in.at[k], q_recv.at[k])
         o = other_of(k)
         landed(kv_in.at[o], kv_recv.at[o])
+        return carry
+
+    def forward(n, carry):
+        k = jnp.where(upward, n, 3 - n)
+        i = mine_of(k)
+
+        @pl.when(jnp.logical_and(n < 3, upward))
+        def _():
+            take(n + 1)
+
+        first = jnp.where(upward, n, 0)
+        lax.fori_loop(first, jnp.where(upward, n + 1, jnp.where(n == 0, 4, 0)), arrive, 0)
         m_acc[...] = forward_pair(k, i, True)
 
         def inner(j, c):
@@ -449,9 +459,14 @@
             dm_out[h, rows, :] = dm[:, h * HEAD : (h + 1) * HEAD]
         return carry
 
-    lax.fori_loop(0, TOK // TILE, post_tile, 0)
-    for h in far_first:
-        push(dm_out.at[h], dm_in.at[slot_of_s], dm_send.at[h], dm_recv.at[slot_of_s], *worker(h))
+    for part in range(2):
+        lax.fori_loop(2 * part, 2 * part + 2, post_tile, 0)
+        rows = pl.ds(part * 256, 256)
+        for h in far_first:
+            push(
+                dm_out.at[h, rows], dm_in.at[slot_of_s, rows], dm_send.at[h, part], dm_recv.at[slot_of_s, part],
+                *worker(h),
+            )
 
     terms[4] = (dot(joined[...], upstream[...], 0, 0) * factor).astype(BF)
     terms[0] = (dot(normed_t[...], pback[:, :WIDTH]) * factor).astype(BF)
@@ -463,7 +478,8 @@
         step(u, 1)
 
     for k in range(4):
-        landed(dm_in.at[k], dm_recv.at[k])
+        for part in range(2):
+            landed(dm_in.at[k, pl.ds(part * 256, 256)], dm_recv.at[k, part])
 
     def backward_pair(k, j, diagonal):
         q, dm = q_in[k], dm_in[k]
@@ -601,7 +617,7 @@
         q = lax.rem(s + p, 8)
         rows = pl.ds(pl.multiple_of(q * 256, 256), 256)
         found[rows, :] = (dot(put_one[rows, :], egrad[:, :256]) + dot(put_two[rows, :], egrad[:, 256:])).astype(BF)
-        spread(found, incoming_ref, back_send, back_recv, s, t, q, sixteen)
+        spread(found, incoming, back_send, back_recv, s, t, q, sixteen)
         return carry
 
     for n in range(4):
@@ -611,10 +627,20 @@
         if n < 3:
             for u in EARLY:
                 step(u, n + 6)
-    for n in range(7, 9):
-        for u in LATE:
-            step(u, n)
-    landed(incoming_ref, back_recv)
+    for u in LATE:
+        step(u, 7)
+    landed(incoming, back_recv)
+
+    def order_tile(q, carry):
+        both = incoming[pl.ds(pl.multiple_of(q * 256, 256), 256), :].astype(F32).reshape(16, 16, 256)
+        part = pl.ds(pl.multiple_of(q * 128, 128), 128)
+        rows_ref[part, :256] = both[:, :SLOTS].reshape(128, 256).astype(BF)
+        rows_ref[part, 256:] = both[:, SLOTS:].reshape(128, 256).astype(BF)
+        return carry
+
+    lax.fori_loop(0, 8, order_tile, 0)
+    for u in LATE:
+        step(u, 8)
     landed(found.at[pl.ds(0, (OWNERS - 1) * 16)], back_send)
     landed(req_out.at[pl.ds(0, OWNERS - 1)], req_send)
 
@@ -622,7 +648,8 @@
         to = worker(h)
         left(kv_out.at[h], kv_send.at[h], *to)
         left(q_out.at[h], q_send.at[h], *to)
-        left(dm_out.at[h], dm_send.at[h], *to)
+        for part in range(2):
+            left(dm_out.at[h, pl.ds(part * 256, 256)], dm_send.at[h, part], *to)
         landed(kv_in.at[mine_of(h)], fwd_send.at[h])
         landed(part_out.at[h], part_send.at[h])
         back = (mine_of(h), base + user_core)
@@ -657,7 +684,7 @@
     heads, pairs, carried = buf(4, TOK, HEAD), buf(4, TOK, 2 * HEAD), buf(4, TOK + 16, HEAD)
     message = buf(OWNERS, 1, 128, dtype=F32)
     blocks = [
-        buf(ROWS, WIDTH), square, buf(WIDTH, 4 * WIDTH), square,
+        buf(ROWS, WIDTH), square, buf(WIDTH, 4 * WIDTH), square, buf(ROWS, 256),
         square, square, buf(n, WIDTH, WIDTH), square, square, buf(TOK, 4 * WIDTH, dtype=F32), square, square,
         square, wide, wide, buf(TOK, 4 * WIDTH),
         heads, pairs, heads, buf(8, TOK, 2 * HEAD), carried, carried, heads, heads,
@@ -669,13 +696,13 @@
         buf(n, 3, 16, WIDTH), buf(n, 16, WIDTH), buf(n, 3, 16, 128),
     ]
     one, three = dma((n,)), dma((n, 3))
-    sems = [dma((c,)) for c in (4, 4, 4, 8, 4, 4, 4, 4, 4, 4, 4, 4, 4, 4, 4)]
+    sems = [dma((c,)) for c in (4, 4, 4, 8, 4, 4, 4)] + [dma((4, 2))] * 2 + [dma((4,))] * 6
     sems += [dma((4,))] + [dma] * 6 + [one] * 2 + [three] * 12 + [one] * 2
     return pl.pallas_call(
         functools.partial(step_kernel, factor),
         out_shape=(
             jax.ShapeDtypeStruct((TOK, WIDTH), BF),
-            jax.ShapeDtypeStruct((ROWS, 256), BF),
+            jax.ShapeDtypeStruct((OWNERS * SLOTS, WIDTH), BF),
             jax.ShapeDtypeStruct((n, WIDTH, WIDTH), BF),
             jax.ShapeDtypeStruct((8, OWNERS * SLOTS), F32),
         ),
@@ -688,24 +715,16 @@
     )(length, owner, item_row, item_table, out_grad, gain_in.reshape(1, -1), gain_out.reshape(1, -1), w_in, w_out)
 
 
-def finish_kernel(incoming_ref, asked_ref, sums_ref, out_ref, w_in_ref, w_out_ref, rows):
-    @pl.when(pl.program_id(0) == 0)
-    def _():
-        for q in range(8):
-            both = incoming_ref[q * 256 : (q + 1) * 256, :].astype(F32).reshape(16, 16, 256)
-            part = slice(q * 128, (q + 1) * 128)
-            rows[part, :256] = both[:, :SLOTS].reshape(128, 256).astype(BF)
-            rows[part, 256:] = both[:, SLOTS:].reshape(128, 256).astype(BF)
-
+def finish_kernel(rows_ref, asked_ref, sums_ref, out_ref, w_in_ref, w_out_ref):
     at = lax.broadcasted_iota(jnp.int32, (256, OWNERS * SLOTS), 0) + pl.program_id(0) * 256
     hit = at == asked_ref[...][:1].astype(jnp.int32)
-    out_ref[...] = dot(jnp.where(hit, 1.0, 0.0).astype(BF), rows[...])
+    out_ref[...] = dot(jnp.where(hit, 1.0, 0.0).astype(BF), rows_ref[...])
     for u in range(4):
         w_in_ref[:, u * WIDTH : (u + 1) * WIDTH] = sums_ref[u].astype(F32)
     w_out_ref[...] = sums_ref[4].astype(F32)
 
 
-def finish(incoming, asked, sums):
+def finish(rows, asked, sums):
     n = len(ORDERS)
     return pl.pallas_call(
         finish_kernel,
@@ -716,7 +735,7 @@
             jax.ShapeDtypeStruct((WIDTH, WIDTH), F32),
         ),
         in_specs=[
-            pl.BlockSpec((ROWS, 256), lambda i: (0, 0)),
+            pl.BlockSpec((OWNERS * SLOTS, WIDTH), lambda i: (0, 0)),
             pl.BlockSpec((8, OWNERS * SLOTS), lambda i: (0, 0)),
             pl.BlockSpec((n, 64, WIDTH), lambda i: (0, i, 0)),
         ],
@@ -725,17 +744,16 @@
             pl.BlockSpec((64, 4 * WIDTH), lambda i: (i, 0)),
             pl.BlockSpec((64, WIDTH), lambda i: (i, 0)),
         ),
-        scratch_shapes=[pltpu.VMEM((OWNERS * SLOTS, WIDTH), BF)],
         compiler_params=pltpu.CompilerParams(vmem_limit_bytes=60 * 1024 * 1024),
-    )(incoming, asked, sums)
+    )(rows, asked, sums)
 
 
 def local(item_table, owner, item_row, lengths, gain_in, gain_out, w_in, w_out, out_grad):
     factor = (TOK * OWNERS) ** (-0.5)
-    hidden, incoming, sums, asked = layer_step(
+    hidden, rows, sums, asked = layer_step(
         lengths, owner.reshape(1, TOK), item_row, item_table, out_grad[0], gain_in, gain_out, w_in, w_out, factor
     )
-    table_grad, w_in_grad, w_out_grad = finish(incoming, asked, sums)
+    table_grad, w_in_grad, w_out_grad = finish(rows, asked, sums)
     return (hidden[None], table_grad, w_in_grad, w_out_grad)
 
 

time: 177 us -> 176 us (level)
  no operation moved by 1% of the time
where the time goes in v7:
time: 176 us
  Pallas kernels  174 us (99%)
    pallas_call x1, Pallas kernels, layer_step(): pl.pallas_call(functools.partial(step_kernel, factor), out_shape=(jax.Sha...  165 us
    pallas_call x1, Pallas kernels, finish(): pl.pallas_call(finish_kernel, grid=(8,), out_shape=(jax.ShapeDtypeStruct(...  8.78 us

profile of v7, /device:TPU:1, one launch (start us, length us, event | category | flops | bytes accessed | tf_op | source)
XLA Modules:
  0.0 175.7 jit_solution(2576917523240968481)
XLA Ops:
  1.3 164.8 %shard_map.120 = (bf16[512,512]{1,0:T(8,128)(2,1)}, bf16[1024,512]{1,0:T(8,128)(2,1)}, bf16[5,512,512]{2,1,0:T(8,128)(2,1)}, f32[8,1024]{1,0:T(8,128)}) custom-call(s32[1]{0:T(128)S(6)} %copy.14.len_ref, s32[1,512]{1,0:T(1,128)} %bitcast.7, s32[1,512]{1,0:T(1,128)} %row_ref.1, bf16[2048,512]{1,0:T(8,128)(2,1)} %table_hbm.1, bf16[512,512]{1,0:T(8,128)(2,1)} %bitcast.6, ...), custom_call_target="tpu_custom_call" | custom-call | tf_op jit(solution)/shard_map/pallas_call | solution.py:701
  166.1 0.0 copy-start
  166.1 8.8 %shard_map.121 = (f32[2048,512]{1,0:T(8,128)}, f32[512,2048]{1,0:T(8,128)}, f32[512,512]{1,0:T(8,128)}) custom-call(bf16[1024,512]{1,0:T(8,128)(2,1)} %get-tuple-element.12.rows_ref, f32[8,1024]{1,0:T(8,128)} %get-tuple-element.13.asked_ref, bf16[5,512,512]{2,1,0:T(8,128)(2,1)} %get-tuple-element.14.sums_ref), custom_call_target="tpu_custom_call" | custom-call | tf_op jit(solution)/shard_map/pallas_call | solution.py:729
  174.9 0.0 copy-done
  174.9 0.8 copy.15
Async XLA Ops:
  166.1 8.8 %copy-start = (bf16[512,512]{1,0:T(8,128)(2,1)S(1)}, bf16[512,512]{1,0:T(8,128)(2,1)}, u32[]{:S(2)}) copy-start(bf16[512,512]{1,0:T(8,128)(2,1)} %get-tuple-element.11) | copy-start | bytes 1572868

commit v8 on v7

--- a/solution.py
+++ b/solution.py
@@ -715,8 +715,9 @@
     )(length, owner, item_row, item_table, out_grad, gain_in.reshape(1, -1), gain_out.reshape(1, -1), w_in, w_out)
 
 
-def finish_kernel(rows_ref, asked_ref, sums_ref, out_ref, w_in_ref, w_out_ref):
-    at = lax.broadcasted_iota(jnp.int32, (256, OWNERS * SLOTS), 0) + pl.program_id(0) * 256
+def finish_kernel(rows_ref, asked_ref, sums_ref, layer_ref, out_ref, w_in_ref, w_out_ref, hidden_ref):
+    hidden_ref[...] = layer_ref[...]
+    at = lax.broadcasted_iota(jnp.int32, (1024, OWNERS * SLOTS), 0) + pl.program_id(0) * 1024
     hit = at == asked_ref[...][:1].astype(jnp.int32)
     out_ref[...] = dot(jnp.where(hit, 1.0, 0.0).astype(BF), rows_ref[...])
     for u in range(4):
@@ -724,28 +725,31 @@
     w_out_ref[...] = sums_ref[4].astype(F32)
 
 
-def finish(rows, asked, sums):
+def finish(rows, asked, sums, hidden):
     n = len(ORDERS)
     return pl.pallas_call(
         finish_kernel,
-        grid=(8,),
+        grid=(2,),
         out_shape=(
             jax.ShapeDtypeStruct((ROWS, WIDTH), F32),
             jax.ShapeDtypeStruct((WIDTH, 4 * WIDTH), F32),
             jax.ShapeDtypeStruct((WIDTH, WIDTH), F32),
+            jax.ShapeDtypeStruct((TOK, WIDTH), BF),
         ),
         in_specs=[
             pl.BlockSpec((OWNERS * SLOTS, WIDTH), lambda i: (0, 0)),
             pl.BlockSpec((8, OWNERS * SLOTS), lambda i: (0, 0)),
-            pl.BlockSpec((n, 64, WIDTH), lambda i: (0, i, 0)),
+            pl.BlockSpec((n, 256, WIDTH), lambda i: (0, i, 0)),
+            pl.BlockSpec((256, WIDTH), lambda i: (i, 0)),
         ],
         out_specs=(
+            pl.BlockSpec((1024, WIDTH), lambda i: (i, 0)),
+            pl.BlockSpec((256, 4 * WIDTH), lambda i: (i, 0)),
             pl.BlockSpec((256, WIDTH), lambda i: (i, 0)),
-            pl.BlockSpec((64, 4 * WIDTH), lambda i: (i, 0)),
-            pl.BlockSpec((64, WIDTH), lambda i: (i, 0)),
+            pl.BlockSpec((256, WIDTH), lambda i: (i, 0)),
         ),
         compiler_params=pltpu.CompilerParams(vmem_limit_bytes=60 * 1024 * 1024),
-    )(rows, asked, sums)
+    )(rows, asked, sums, hidden)
 
 
 def local(item_table, owner, item_row, lengths, gain_in, gain_out, w_in, w_out, out_grad):
@@ -753,7 +757,7 @@
     hidden, rows, sums, asked = layer_step(
         lengths, owner.reshape(1, TOK), item_row, item_table, out_grad[0], gain_in, gain_out, w_in, w_out, factor
     )
-    table_grad, w_in_grad, w_out_grad = finish(rows, asked, sums)
+    table_grad, w_in_grad, w_out_grad, hidden = finish(rows, asked, sums, hidden)
     return (hidden[None], table_grad, w_in_grad, w_out_grad)
 
 

time: 176 us -> 173 us (0.983)
  Pallas kernels: 174 us -> 172 us
    pallas_call x1, Pallas kernels: 8.78 us -> 6.84 us  [finish(): pl.pallas_call(finish_kernel, grid=(2,), out_shape=(jax.ShapeDtypeStruct(...]
where the time goes in v8:
time: 173 us
  Pallas kernels  172 us (99%)
    pallas_call x1, Pallas kernels, layer_step(): pl.pallas_call(functools.partial(step_kernel, factor), out_shape=(jax.Sha...  165 us
    pallas_call x1, Pallas kernels, finish(): pl.pallas_call(finish_kernel, grid=(2,), out_shape=(jax.ShapeDtypeStruct(...  6.84 us

profile of v8, /device:TPU:1, one launch (start us, length us, event | category | flops | bytes accessed | tf_op | source)
XLA Modules:
  0.0 173.0 jit_solution(1339571364962988020)
XLA Ops:
  1.3 164.8 %shard_map.120 = (bf16[512,512]{1,0:T(8,128)(2,1)}, bf16[1024,512]{1,0:T(8,128)(2,1)}, bf16[5,512,512]{2,1,0:T(8,128)(2,1)}, f32[8,1024]{1,0:T(8,128)}) custom-call(s32[1]{0:T(128)S(6)} %copy.13.len_ref, s32[1,512]{1,0:T(1,128)} %bitcast.6, s32[1,512]{1,0:T(1,128)} %row_ref.1, bf16[2048,512]{1,0:T(8,128)(2,1)} %table_hbm.1, bf16[512,512]{1,0:T(8,128)(2,1)} %bitcast.5, ...), custom_call_target="tpu_custom_call" | custom-call | tf_op jit(solution)/shard_map/pallas_call | solution.py:701
  166.1 6.8 %shard_map.121 = (f32[2048,512]{1,0:T(8,128)}, f32[512,2048]{1,0:T(8,128)}, f32[512,512]{1,0:T(8,128)}, bf16[512,512]{1,0:T(8,128)(2,1)}) custom-call(bf16[1024,512]{1,0:T(8,128)(2,1)} %get-tuple-element.12.rows_ref, f32[8,1024]{1,0:T(8,128)} %get-tuple-element.13.asked_ref, bf16[5,512,512]{2,1,0:T(8,128)(2,1)} %get-tuple-element.14.sums_ref, ...), custom_call_target="tpu_custom_call" | custom-call | tf_op jit(solution)/shard_map/pallas_call | solution.py:730

commit v9 on v8

--- a/solution.py
+++ b/solution.py
@@ -301,18 +301,24 @@
     copies[0].wait()
 
     def gather(p, carry):
-        q = lax.rem(s + p, 8)
-        column = asked_col[pl.ds(pl.multiple_of(q * 128, 128), 128), :][:, :1].astype(jnp.int32)
-        hit = lax.broadcasted_iota(jnp.int32, (128, ROWS), 1) == column
+        q = lax.rem(s // 2 + p, 4)
+        column = asked_col[pl.ds(pl.multiple_of(q * 256, 256), 256), :][:, :1].astype(jnp.int32)
+        hit = lax.broadcasted_iota(jnp.int32, (256, ROWS), 1) == column
         rows = dot(jnp.where(hit, 1.0, 0.0).astype(BF), table_ref[...])
         both = jnp.concatenate(
-            [rows[:, :256].reshape(16, SLOTS, 256), rows[:, 256:].reshape(16, SLOTS, 256)], axis=1
+            [rows[:, :256].reshape(32, SLOTS, 256), rows[:, 256:].reshape(32, SLOTS, 256)], axis=1
         )
-        found[pl.ds(pl.multiple_of(q * 256, 256), 256), :] = both.reshape(256, 256).astype(BF)
-        spread(found, fetched, row_send, row_recv, s, t, q, sixteen)
-        return carry
-
-    lax.fori_loop(0, 8, gather, 0)
+        found[pl.ds(pl.multiple_of(q * 512, 512), 512), :] = both.reshape(512, 256).astype(BF)
+
+        def side(e, c):
+            spread(found, fetched, row_send, row_recv, s, t, 2 * q + lax.rem(s + e, 2), sixteen)
+            return c
+
+        lax.fori_loop(0, 2, side, 0)
+        return carry
+
+    lax.fori_loop(0, 4, gather, 0)
+
     def pick_tile(r, carry):
         rows = pl.ds(pl.multiple_of(r * TILE, TILE), TILE)
         at = lax.broadcasted_iota(jnp.int32, (TILE, ROWS), 1)
@@ -327,10 +333,11 @@
     copies[3].wait()
     landed(fetched, row_recv)
 
+    x_ref[:, :256] = dot(pick_one[...], fetched[...]).astype(BF)
+    x_ref[:, 256:] = dot(pick_two[...], fetched[...]).astype(BF)
+
     def norm_tile(r, carry):
         rows = pl.ds(pl.multiple_of(r * TILE, TILE), TILE)
-        x_ref[rows, :256] = dot(pick_one[rows, :], fetched[...]).astype(BF)
-        x_ref[rows, 256:] = dot(pick_two[rows, :], fetched[...]).astype(BF)
         x = x_ref[rows, :].astype(F32)
         mean = jnp.mean(x, -1, keepdims=True)
         cent = x - mean
@@ -588,7 +595,7 @@
 
     def back_tile(r, carry):
         rows = pl.ds(pl.multiple_of(r * TILE, TILE), TILE)
-        nb = nback[rows, :] + dot(pback[rows, WIDTH:], w_in_ref[:, WIDTH:], 1, 1)
+        nb = nback[rows, :]
         x = x_ref[rows, :].astype(F32)
         mean = jnp.mean(x, -1, keepdims=True)
         cent = x - mean
@@ -600,11 +607,13 @@
         egrad[rows, :] = (dx + upstream[rows, :].astype(F32)).astype(BF)
         return carry
 
+    nback[:256, :] += dot(pback[:256, WIDTH:], w_in_ref[:, WIDTH:], 1, 1)
     lax.fori_loop(0, 2, back_tile, 0)
     for u in LATE:
         step(u, 1)
     for u in EARLY:
         step(u, 4)
+    nback[256:, :] += dot(pback[256:, WIDTH:], w_in_ref[:, WIDTH:], 1, 1)
     lax.fori_loop(2, 4, back_tile, 0)
     for u in LATE:
         step(u, 2)

time: 173 us -> 171 us (0.988)
  Pallas kernels: 172 us -> 170 us
    pallas_call x1, Pallas kernels: 165 us -> 163 us  [layer_step(): pl.pallas_call(functools.partial(step_kernel, factor), out_shape=(jax.Sha...]
where the time goes in v9:
time: 171 us
  Pallas kernels  170 us (99%)
    pallas_call x1, Pallas kernels, layer_step(): pl.pallas_call(functools.partial(step_kernel, factor), out_shape=(jax.Sha...  163 us
    pallas_call x1, Pallas kernels, finish(): pl.pallas_call(finish_kernel, grid=(2,), out_shape=(jax.ShapeDtypeStruct(...  6.85 us

profile of v9, /device:TPU:1, one launch (start us, length us, event | category | flops | bytes accessed | tf_op | source)
XLA Modules:
  0.0 171.1 jit_solution(1340737094716554125)
XLA Ops:
  1.3 162.9 %shard_map.120 = (bf16[512,512]{1,0:T(8,128)(2,1)}, bf16[1024,512]{1,0:T(8,128)(2,1)}, bf16[5,512,512]{2,1,0:T(8,128)(2,1)}, f32[8,1024]{1,0:T(8,128)}) custom-call(s32[1]{0:T(128)S(6)} %copy.13.len_ref, s32[1,512]{1,0:T(1,128)} %bitcast.6, s32[1,512]{1,0:T(1,128)} %row_ref.1, bf16[2048,512]{1,0:T(8,128)(2,1)} %table_hbm.1, bf16[512,512]{1,0:T(8,128)(2,1)} %bitcast.5, ...), custom_call_target="tpu_custom_call" | custom-call | tf_op jit(solution)/shard_map/pallas_call | solution.py:710
  164.2 6.8 %shard_map.121 = (f32[2048,512]{1,0:T(8,128)}, f32[512,2048]{1,0:T(8,128)}, f32[512,512]{1,0:T(8,128)}, bf16[512,512]{1,0:T(8,128)(2,1)}) custom-call(bf16[1024,512]{1,0:T(8,128)(2,1)} %get-tuple-element.12.rows_ref, f32[8,1024]{1,0:T(8,128)} %get-tuple-element.13.asked_ref, bf16[5,512,512]{2,1,0:T(8,128)(2,1)} %get-tuple-element.14.sums_ref, ...), custom_call_target="tpu_custom_call" | custom-call | tf_op jit(solution)/shard_map/pallas_call | solution.py:739

commit v10 on v9

--- a/solution.py
+++ b/solution.py
@@ -623,14 +623,19 @@
     landed(found.at[pl.ds(0, (OWNERS - 1) * 16)], row_send)
 
     def scatter(p, carry):
-        q = lax.rem(s + p, 8)
-        rows = pl.ds(pl.multiple_of(q * 256, 256), 256)
+        q = lax.rem(s // 2 + p, 4)
+        rows = pl.ds(pl.multiple_of(q * 512, 512), 512)
         found[rows, :] = (dot(put_one[rows, :], egrad[:, :256]) + dot(put_two[rows, :], egrad[:, 256:])).astype(BF)
-        spread(found, incoming, back_send, back_recv, s, t, q, sixteen)
+
+        def side(e, c):
+            spread(found, incoming, back_send, back_recv, s, t, 2 * q + lax.rem(s + e, 2), sixteen)
+            return c
+
+        lax.fori_loop(0, 2, side, 0)
         return carry
 
     for n in range(4):
-        lax.fori_loop(2 * n, 2 * n + 2, scatter, 0)
+        scatter(n, 0)
         for u in LATE:
             step(u, n + 3)
         if n < 3:

time: 171 us -> 172 us (level)
  no operation moved by 1% of the time
where the time goes in v10:
time: 172 us
  Pallas kernels  171 us (99%)
    pallas_call x1, Pallas kernels, layer_step(): pl.pallas_call(functools.partial(step_kernel, factor), out_shape=(jax.Sha...  164 us
    pallas_call x1, Pallas kernels, finish(): pl.pallas_call(finish_kernel, grid=(2,), out_shape=(jax.ShapeDtypeStruct(...  6.84 us

profile of v10, /device:TPU:1, one launch (start us, length us, event | category | flops | bytes accessed | tf_op | source)
XLA Modules:
  0.0 172.3 jit_solution(14197037483408967266)
XLA Ops:
  1.3 164.1 %shard_map.120 = (bf16[512,512]{1,0:T(8,128)(2,1)}, bf16[1024,512]{1,0:T(8,128)(2,1)}, bf16[5,512,512]{2,1,0:T(8,128)(2,1)}, f32[8,1024]{1,0:T(8,128)}) custom-call(s32[1]{0:T(128)S(6)} %copy.13.len_ref, s32[1,512]{1,0:T(1,128)} %bitcast.6, s32[1,512]{1,0:T(1,128)} %row_ref.1, bf16[2048,512]{1,0:T(8,128)(2,1)} %table_hbm.1, bf16[512,512]{1,0:T(8,128)(2,1)} %bitcast.5, ...), custom_call_target="tpu_custom_call" | custom-call | tf_op jit(solution)/shard_map/pallas_call | solution.py:715
  165.4 6.8 %shard_map.121 = (f32[2048,512]{1,0:T(8,128)}, f32[512,2048]{1,0:T(8,128)}, f32[512,512]{1,0:T(8,128)}, bf16[512,512]{1,0:T(8,128)(2,1)}) custom-call(bf16[1024,512]{1,0:T(8,128)(2,1)} %get-tuple-element.12.rows_ref, f32[8,1024]{1,0:T(8,128)} %get-tuple-element.13.asked_ref, bf16[5,512,512]{2,1,0:T(8,128)(2,1)} %get-tuple-element.14.sums_ref, ...), custom_call_target="tpu_custom_call" | custom-call | tf_op jit(solution)/shard_map/pallas_call | solution.py:744
